TPU v7x, 256 devices: a whole 4x4x8 slice. The times are simulated.
256 devices in a mesh: grp: 8 (over y, x_lo), sp: 32 (over x_hi, z, core).
Axes of the slice: x: 4 (x_hi: 2, x_lo: 2; x = x_hi * 2 + x_lo), y: 4, z: 8, core: 2. Of those that a mesh axis runs over, the one named last changes fastest.
Arguments:
- fields: bfloat16 [8, 128, 16, 16, 192], P('grp', 'sp'), may hold values from -6 to 6
- depth_kernel: float32 [7, 7, 192], replicated, may hold values from -0.875 to 0.875
- layer_norm_gain: float32 [192], replicated, may hold values from 0.1 to 1.9
- layer_norm_bias: float32 [192], replicated, may hold values from -3 to 3
- up_weight: bfloat16 [192, 768], replicated, may hold values from -0.4375 to 0.4375
- up_bias: float32 [768], replicated, may hold values from -3 to 3
- down_weight: bfloat16 [768, 192], replicated, may hold values from -0.21875 to 0.21875
- cotangent: bfloat16 [8, 128, 16, 16, 192], P('grp', 'sp'), may hold values from -6 to 6
- neighbours: int32 [128, 8], replicated, may hold values from 0 to 127, as said below
- rotation: int32 [128, 8], replicated, may hold values from 0 to 3, as said below
- tile_owner: int32 [128], replicated, may hold values from 0 to 127, as said below
Outputs:
- updated: bfloat16 [8, 128, 16, 16, 192], P('grp', 'sp')
- grad_fields: bfloat16 [8, 128, 16, 16, 192], P('grp', 'sp')
- grad_kernel: float32 [7, 7, 192], replicated
- grad_gain: float32 [192], replicated
- grad_bias: float32 [192], replicated
- grad_up_weight: float32 [192, 768], replicated
- grad_up_bias: float32 [768], replicated
- grad_down_weight: float32 [768, 192], replicated
Inputs may be any that keep to these rules, and one draw needn't show every extreme that they name: neighbours[q, s] is the tile beside tile q in slot s, and the relation is mutual (top with bottom, left with right, each corner with the opposite one). For the tile in storage row p, every neighbour's storage row lies in block p // 4 - 1, p // 4 or p // 4 + 1 (blocks of 4 rows, counted cyclically over 32 blocks). `rotation`: quarter turns counterclockwise applied to the neighbour tile before its border is read; the turn that tile q gives its neighbour and the turn that the neighbour gives q add up to a multiple of 4. `tile_owner`: a permutation of the storage rows.
All inputs are finite; a program needn't handle non-finite values.
Results may differ from a plain program's by a relative error of at most 0.0056.
Values may be sent and summed in bfloat16 or wider, within the bound.
No kernel may reach another device: no remote copies, remote signals or barrier semaphores. Data moves between devices by JAX's collectives and lax.ppermute only.
A program may use at most 128 MiB of HBM per device.

v0:
```python
import math

import jax
import jax.numpy as jnp
from jax import lax
from jax.sharding import PartitionSpec as P

GELU_C = math.sqrt(2.0 / math.pi)
EPSILON = 1e-06
SIDE_OF_SLOT = (2, 0, 3, 1)
CORNER_OF_SLOT = (2, 1, 3, 0)


def with_halo(cells, sides, width):
    for axis, dim in sides:
        count = lax.axis_size(axis)
        head = lax.slice_in_dim(cells, 0, width, axis=dim)
        tail = lax.slice_in_dim(cells, cells.shape[dim] - width, cells.shape[dim], axis=dim)
        cells = jnp.concatenate(
            [
                lax.ppermute(tail, axis, [(i, (i + 1) % count) for i in range(count)]),
                cells,
                lax.ppermute(head, axis, [((i + 1) % count, i) for i in range(count)]),
            ],
            axis=dim,
        )
    return cells


def as_sent(x):

    def short(part):
        return part.astype(jnp.bfloat16) if part.dtype == jnp.float32 else part

    return jax.tree.map(short, x)


def passed_along(x, axis, by):
    count = lax.axis_size(axis)
    return lax.ppermute(x, axis, [(i, (i + by) % count) for i in range(count)])


def gelu_pair(value):
    cubic = 0.044715 * value * value * value
    tangent = jnp.tanh(GELU_C * (value + cubic))
    result = 0.5 * value * (1.0 + tangent)
    slope = 0.5 * (1.0 + tangent) + 0.5 * value * (1.0 - tangent * tangent) * GELU_C * (
        1.0 + 3.0 * 0.044715 * value * value
    )
    return (result, slope)


def border_stack(tiles):
    tile_side = tiles.shape[1]
    return jnp.stack(
        [
            tiles[:, :3],
            jnp.swapaxes(tiles[:, :, :3], 1, 2),
            tiles[:, tile_side - 3 :],
            jnp.swapaxes(tiles[:, :, tile_side - 3 :], 1, 2),
        ],
        axis=1,
    )


def side_region(strip_stack, strip_index):
    strip_piece = strip_stack[:, strip_index]
    if strip_index % 2 == 1:
        strip_piece = jnp.swapaxes(strip_piece, 1, 2)
    return strip_piece


def corner_region(strip_stack, corner_index):
    tile_side = strip_stack.shape[3]
    source = strip_stack[:, 0] if corner_index in (0, 3) else strip_stack[:, 2]
    if corner_index in (0, 1):
        return source[:, :, :3]
    return source[:, :, tile_side - 3 :]


def rotate_select(candidates, quarter_turns):
    result = candidates[0]
    for quarter in range(1, 4):
        result = jnp.where(
            (quarter_turns == quarter)[:, None, None, None], candidates[quarter], result
        )
    return result


def slot_band(strip_stack, quarter_turns, slot_number):
    if slot_number < 4:
        target = SIDE_OF_SLOT[slot_number]
        options = [
            jnp.rot90(side_region(strip_stack, (target - quarter) % 4), quarter, axes=(1, 2))
            for quarter in range(4)
        ]
    else:
        target = CORNER_OF_SLOT[slot_number - 4]
        options = [
            jnp.rot90(corner_region(strip_stack, (target - quarter) % 4), quarter, axes=(1, 2))
            for quarter in range(4)
        ]
    return rotate_select(options, quarter_turns)


def assemble_padded(sample, bands):
    upper = jnp.concatenate([bands[4], bands[0], bands[5]], axis=2)
    middle = jnp.concatenate([bands[2], sample, bands[3]], axis=2)
    lower = jnp.concatenate([bands[6], bands[1], bands[7]], axis=2)
    return jnp.concatenate([upper, middle, lower], axis=1)


def place_side(region, strip_index):
    strip_piece = jnp.swapaxes(region, 1, 2) if strip_index % 2 == 1 else region
    pieces = [jnp.zeros_like(strip_piece) for _ in range(4)]
    pieces[strip_index] = strip_piece
    return jnp.stack(pieces, axis=1)


def place_corner(region, corner_index, tile_side):
    before = 0 if corner_index in (0, 1) else tile_side - 3
    strip_piece = jnp.pad(region, ((0, 0), (0, 0), (before, tile_side - 3 - before), (0, 0)))
    pieces = [jnp.zeros_like(strip_piece) for _ in range(4)]
    pieces[0 if corner_index in (0, 3) else 2] = strip_piece
    return jnp.stack(pieces, axis=1)


def slot_return(region, quarter_turns, slot_number, tile_side):
    result = None
    for quarter in range(4):
        back = jnp.rot90(region, (4 - quarter) % 4, axes=(1, 2))
        if slot_number < 4:
            piece = place_side(back, (SIDE_OF_SLOT[slot_number] - quarter) % 4)
        else:
            piece = place_corner(back, (CORNER_OF_SLOT[slot_number - 4] - quarter) % 4, tile_side)
        weight = (quarter_turns == quarter).astype(jnp.float32)[:, None, None, None, None]
        result = weight * piece if result is None else result + weight * piece
    return result


def cycle_regions(grad_pad, tile_side):
    edge = tile_side + 3
    return [
        grad_pad[:, 0:3, 3:edge],
        grad_pad[:, edge:, 3:edge],
        grad_pad[:, 3:edge, 0:3],
        grad_pad[:, 3:edge, edge:],
        grad_pad[:, :3, :3],
        grad_pad[:, :3, edge:],
        grad_pad[:, edge:, :3],
        grad_pad[:, edge:, edge:],
    ]


def strips_to_tile(strip_stack, tile_side):
    rest = tile_side - 3
    top_part = jnp.pad(strip_stack[:, 0], ((0, 0), (0, rest), (0, 0), (0, 0)))
    left_part = jnp.pad(jnp.swapaxes(strip_stack[:, 1], 1, 2), ((0, 0), (0, 0), (0, rest), (0, 0)))
    bottom_part = jnp.pad(strip_stack[:, 2], ((0, 0), (rest, 0), (0, 0), (0, 0)))
    right_part = jnp.pad(jnp.swapaxes(strip_stack[:, 3], 1, 2), ((0, 0), (0, 0), (rest, 0), (0, 0)))
    return top_part + left_part + bottom_part + right_part


def on_device(
    fields,
    depth_kernel,
    layer_norm_gain,
    layer_norm_bias,
    up_weight,
    up_bias,
    down_weight,
    cotangent,
    neighbours,
    rotation,
    tile_owner,
):
    tiles_here = fields.shape[1]
    tile_side = fields.shape[2]
    channels = fields.shape[4]
    axis_length = lax.axis_size("sp")
    position = lax.axis_index("sp")
    tile_total = neighbours.shape[0]
    scale = 1.0 / math.sqrt(lax.axis_size("grp") * axis_length * tiles_here * tile_side * tile_side)
    tile_id = (
        jnp.zeros((tile_total,), jnp.int32)
        .at[tile_owner]
        .set(jnp.arange(tile_total, dtype=jnp.int32))
    )
    own_rows = position * tiles_here + jnp.arange(tiles_here, dtype=jnp.int32)
    own_ids = tile_id[own_rows]
    near_rows = tile_owner[neighbours[own_ids]]
    quarter_turns = rotation[own_ids]
    wide_pos = (
        near_rows // tiles_here - position + 1
    ) % axis_length * tiles_here + near_rows % tiles_here
    sample = fields[0]
    cotan = cotangent[0]
    widened = with_halo(border_stack(sample), (("sp", 0),), tiles_here)
    bands = [
        slot_band(widened[wide_pos[:, slot_number]], quarter_turns[:, slot_number], slot_number)
        for slot_number in range(8)
    ]
    padded = assemble_padded(sample, bands)
    mixed = jnp.zeros(sample.shape, jnp.float32)
    for offset_row in range(7):
        for offset_col in range(7):
            mixed = (
                mixed
                + padded[
                    :, offset_row : offset_row + tile_side, offset_col : offset_col + tile_side, :
                ].astype(jnp.float32)
                * depth_kernel[offset_row, offset_col]
            )
    average = jnp.mean(mixed, axis=-1, keepdims=True)
    mean_removed = mixed - average
    variance = jnp.mean(mean_removed * mean_removed, axis=-1, keepdims=True)
    inverse_deviation = lax.rsqrt(variance + EPSILON)
    standardized_input = mean_removed * inverse_deviation
    normalized_output = (standardized_input * layer_norm_gain + layer_norm_bias).astype(
        jnp.bfloat16
    )
    flat_normed = normalized_output.reshape(-1, channels)
    up_value = jnp.dot(flat_normed, up_weight, preferred_element_type=jnp.float32) + up_bias
    gelu_value, gelu_slope = gelu_pair(up_value)
    activation = gelu_value.astype(jnp.bfloat16)
    branch = jnp.dot(activation, down_weight, preferred_element_type=jnp.float32).reshape(
        sample.shape
    )
    updated = (sample.astype(jnp.float32) + branch).astype(jnp.bfloat16)
    flat_cotan = cotan.reshape(-1, channels)
    d_up = jnp.dot(flat_cotan, down_weight.T, preferred_element_type=jnp.float32) * gelu_slope
    d_up_b = d_up.astype(jnp.bfloat16)
    grad_up_b = jnp.sum(d_up, axis=0)
    normalized_gradient = jnp.dot(d_up_b, up_weight.T, preferred_element_type=jnp.float32).reshape(
        sample.shape
    )
    gain_gradient = jnp.sum(normalized_gradient * standardized_input, axis=(0, 1, 2))
    grad_b = jnp.sum(normalized_gradient, axis=(0, 1, 2))
    gain_scaled = normalized_gradient * layer_norm_gain
    mixed_gradient = inverse_deviation * (
        gain_scaled
        - jnp.mean(gain_scaled, axis=-1, keepdims=True)
        - standardized_input * jnp.mean(gain_scaled * standardized_input, axis=-1, keepdims=True)
    )
    spread = jnp.pad(mixed_gradient, ((0, 0), (6, 6), (6, 6), (0, 0)))
    d_padded = jnp.zeros((tiles_here, tile_side + 6, tile_side + 6, channels), jnp.float32)
    kernel_terms = []
    for offset_row in range(7):
        for offset_col in range(7):
            d_padded = (
                d_padded
                + depth_kernel[offset_row, offset_col]
                * spread[
                    :,
                    6 - offset_row : 12 + tile_side - offset_row,
                    6 - offset_col : 12 + tile_side - offset_col,
                    :,
                ]
            )
            kernel_terms.append(
                jnp.sum(
                    padded[
                        :,
                        offset_row : offset_row + tile_side,
                        offset_col : offset_col + tile_side,
                        :,
                    ].astype(jnp.float32)
                    * mixed_gradient,
                    axis=(0, 1, 2),
                )
            )
    grad_k = jnp.stack(kernel_terms).reshape(7, 7, channels)
    regions = cycle_regions(d_padded, tile_side)
    targets = jnp.arange(3 * tiles_here, dtype=jnp.int32)
    collected = jnp.zeros((3 * tiles_here, 4, 3, tile_side, channels), jnp.float32)
    for slot_number in range(8):
        onehot = (wide_pos[:, slot_number][:, None] == targets[None, :]).astype(jnp.float32)
        contribution = slot_return(
            regions[slot_number], quarter_turns[:, slot_number], slot_number, tile_side
        )
        collected = collected + jnp.einsum(
            "te,tabcd->eabcd", onehot, contribution, precision=lax.Precision.HIGHEST
        )
    from_right = passed_along(as_sent(collected[:tiles_here]), "sp", -1)
    from_left = passed_along(as_sent(collected[2 * tiles_here :]), "sp", 1)
    cycle_grad = collected[tiles_here : 2 * tiles_here] + from_right + from_left
    d_sample = d_padded[:, 3 : 3 + tile_side, 3 : 3 + tile_side, :] + strips_to_tile(
        cycle_grad, tile_side
    )
    grad_x = (cotan.astype(jnp.float32) + d_sample).astype(jnp.bfloat16)
    grad_up = jnp.dot(flat_normed.T, d_up_b, preferred_element_type=jnp.float32)
    grad_down = jnp.dot(activation.T, flat_cotan, preferred_element_type=jnp.float32)
    summed = lax.psum((grad_k, gain_gradient, grad_b, grad_up, grad_up_b, grad_down), ("grp", "sp"))
    grad_k, gain_gradient, grad_b, grad_up, grad_up_b, grad_down = summed
    return (
        updated[None],
        grad_x[None],
        grad_k * scale,
        gain_gradient * scale,
        grad_b * scale,
        grad_up * scale,
        grad_up_b * scale,
        grad_down * scale,
    )


def solution(mesh):
    return jax.shard_map(
        on_device,
        mesh=mesh,
        in_specs=(
            P("grp", "sp", None, None, None),
            P(),
            P(),
            P(),
            P(),
            P(),
            P(),
            P("grp", "sp", None, None, None),
            P(),
            P(),
            P(),
        ),
        out_specs=(
            P("grp", "sp", None, None, None),
            P("grp", "sp", None, None, None),
            P(),
            P(),
            P(),
            P(),
            P(),
            P(),
        ),
        check_vma=False,
    )
```

profile of v0, /device:TPU:1, one launch (start us, length us, event | category | flops | bytes accessed | tf_op | source)
XLA Modules:
  0.0 552.3 jit_solution(4090200526861699336)
XLA Ops:
  10.8 3.3 collective-permute-start.1
  61.2 19.9 %fusion.445 = (f32[4,16,16]{0,1,2:T(8,128)S(1)}, f32[4,16,16,192]{3,0,1,2:T(4,128)S(1)}) fusion(f32[192]{0:T(256)S(1)} %bitcast.516, bf16[4,19,22,192]{3,0,1,2:T(4,128)(2,1)S(1)} %get-tuple-element.170, f32[192]{0:T(256)S(1)} %bitcast.518, f32[192]{0:T(256)S(1)} %bitcast.522, f32[192]{0:T(256)S(1)} %bitcast.524, f32[192]{0:T(256)S(1)} %bitcast.526, ...), kind=kLoop, calls=%fused_computation.831 | loop fusion | flops 30080000 | bytes 17883904 | tf_op jit(solution)/shard_map/reduce_sum | solution.py:214
  84.9 3.0 fusion.467
  89.2 2.1 fusion.444
  92.7 3.0 fusion.468
  96.6 2.5 copy.110
  99.1 2.8 multiply_reduce_fusion
  101.9 9.3 %fusion.199 = (f32[192]{0:T(256)S(1)}, f32[192]{0:T(256)S(1)}, f32[192]{0:T(256)S(1)}, f32[192]{0:T(256)S(1)}, f32[192]{0:T(256)S(1)}, /*index=5*/f32[192]{0:T(2...) fusion(bf16[4,19,22,192]{3,0,1,2:T(4,128)(2,1)S(1)} %get-tuple-, ...), kind=kLoop, calls=%fused_computation.421 | loop fusion | flops 11989632 | bytes 9468160 | tf_op jit(solution)/shard_map/reduce_sum | solution.py:261
  111.3 5.3 fusion.169
  117.8 6.3 %fusion.147 = (f32[192]{0:T(256)S(1)}, f32[192]{0:T(256)S(1)}, f32[192]{0:T(256)S(1)}, f32[192]{0:T(256)S(1)}, f32[192]{0:T(256)S(1)}, /*index=5*/f32[192]{0:T(2...) fusion(f32[4,16,16,192]{3,0,1,2:T(4,128)S(1)} %get-tuple-elemen, ...), kind=kLoop, calls=%fused_computation.369 | loop fusion | flops 10613376 | bytes 7878144 | tf_op jit(solution)/shard_map/reduce_sum | solution.py:261
  124.4 46.0 %fusion.95 = f32[4,22,22,192]{3,0,1,2:T(4,128)} fusion(f32[4,16,16,192]{3,0,1,2:T(4,128)S(1)} %get-tuple-element.140, f32[192]{0:T(256)S(1)} %bitcast.517, f32[192]{0:T(256)S(1)} %bitcast.519, f32[192]{0:T(256)S(1)} %bitcast.523, f32[192]{0:T(256)S(1)} %bitcast.525, f32[192]{0:T(256)S(1)} %bitcast.527, f32[192]{0:T(256)S(1)} %bitcast.529, ...), kind=kLoop, calls=%fused_computation.218 | loop fusion | flops 36056064 | bytes 2310912 | tf_op jit(solution)/shard_map/add | solution.py:251
  171.8 2.1 fusion.448
  175.3 84.3 %all-reduce.21 = (f32[7,7,192]{2,1,0:T(8,128)S(1)}, f32[192]{0:T(256)S(1)}, f32[192]{0:T(256)S(1)}, f32[768]{0:T(1024)S(1)}) all-reduce(f32[7,7,192]{2,1,0:T(8,128)S(1)} %reshape.546, f32[192]{0:T(256)S(1)} %get-tuple-element.24, f32[192]{0:T(256)S(1)} %copy-done.164, ...), channel_id=1, replica_groups=mesh['grp'=8,'sp'=32] {'grp','sp'}, use_global_device_ids=true, to_apply=%region_54.55 | all-reduce | flops 10560 | bytes 84480 | tf_op jit(solution)/shard_map/psum | solution.py:293
  265.3 2.1 fusion.227
  267.5 2.1 fusion.235
  269.7 2.1 fusion.243
  271.9 2.2 fusion.206
  274.2 2.2 fusion.211
  276.5 2.3 fusion.221
  279.0 2.2 fusion.217
  281.2 4.6 fusion.466
  289.3 2.2 add_convert_fusion
  291.5 3.3 collective-permute-done.2
  298.7 242.7 %all-reduce.25.cloned.1.call-done = (f32[192,768]{1,0:T(8,128)}, f32[768,192]{0,1:T(8,128)}) async-done(((f32[192,768]{1,0:T(8,128)}, f32[768,192]{0,1:T(8,128)}), (f32[192,768]{1,0:T(8,128)}, f32[768,192]{0,1:T(8,128)})) %all-reduce.25.cloned.1.call-update) | async-done | bytes 1179664 | tf_op jit(solution)/shard_map/psum | solution.py:293
  (593 shorter events, 76.4 us)
Async XLA Ops:
  7.2 76.4 %copy-start = (bf16[192,768]{1,0:T(8,128)(2,1)S(1)}, bf16[192,768]{1,0:T(8,128)(2,1)}, u32[]{:S(2)}) copy-start(bf16[192,768]{1,0:T(8,128)(2,1)} %param.15) | copy-start | bytes 884740
  7.2 534.2 %all-reduce.25.cloned.1.call-start = ((), (), s32[]{:S(2)}) async-start(), calls=%async_computation | async-start | bytes 2359296 | tf_op jit(solution)/shard_map/psum | solution.py:293
  10.2 48.8 %copy-start.5 = (bf16[1,4,16,16,192]{4,1,2,3,0:T(4,128)(2,1)}, bf16[1,4,16,16,192]{4,1,2,3,0:T(4,128)(2,1)S(1)}, u32[]{:S(2)}) copy-start(bf16[1,4,16,16,192]{4,1,2,3,0:T(4,128)(2,1)S(1)} %copy.295) | copy-start | bytes 1179652
  10.8 26.0 %collective-permute-start.1 = (bf16[4,4,3,16,192]{4,0,3,2,1:T(4,128)(2,1)S(1)}, bf16[4,4,3,16,192]{4,0,3,2,1:T(4,128)(2,1)S(1)}, u32[]{:S(2)}, u32[]{:S(2)}) collective-permute-start(bf16[4,4,3,16,192]{4,0,3,2,1:T(4,128)(2,1)S(1)} %pad_maximum_fusion.61), channel_id=1, source_target_pairs={{1,0},{2,1},{3,2},{4,3},{5,4},{6,5},{7,6},{8,7},{9,8},{10,9},{11,1... | collective-permute-start | bytes 884744 | tf_op jit(solution)/shard_map/ppermute | solution.py:23
  14.1 22.7 %collective-permute-start = (bf16[4,4,3,16,192]{4,0,3,2,1:T(4,128)(2,1)S(1)}, bf16[4,4,3,16,192]{4,0,3,2,1:T(4,128)(2,1)S(1)}, u32[]{:S(2)}, u32[]{:S(2)}) collective-permute-start(bf16[4,4,3,16,192]{4,0,3,2,1:T(4,128)(2,1)S(1)} %pad_maximum_fusion.61), channel_id=1, source_target_pairs={{0,1},{1,2},{2,3},{3,4},{4,5},{5,6},{6,7},{7,8},{8,9},{9,10},{10,1... | collective-permute-start | bytes 884744 | tf_op jit(solution)/shard_map/ppermute | solution.py:21
  19.5 18.3 %copy-start.135 = (pred[4]{0:T(512)(128)(4,1)}, pred[4]{0:T(512)(128)(4,1)S(1)}, u32[]{:S(2)}) copy-start(pred[4]{0:T(512)(128)(4,1)S(1)} %get-tuple-element.129) | copy-start | bytes 16
  19.5 18.3 %copy-start.136 = (pred[4]{0:T(512)(128)(4,1)}, pred[4]{0:T(512)(128)(4,1)S(1)}, u32[]{:S(2)}) copy-start(pred[4]{0:T(512)(128)(4,1)S(1)} %get-tuple-element.278) | copy-start | bytes 16
  19.5 18.3 %copy-start.137 = (pred[4]{0:T(512)(128)(4,1)}, pred[4]{0:T(512)(128)(4,1)S(1)}, u32[]{:S(2)}) copy-start(pred[4]{0:T(512)(128)(4,1)S(1)} %get-tuple-element.279) | copy-start | bytes 16
  19.5 18.3 %copy-start.138 = (pred[4]{0:T(512)(128)(4,1)}, pred[4]{0:T(512)(128)(4,1)S(1)}, u32[]{:S(2)}) copy-start(pred[4]{0:T(512)(128)(4,1)S(1)} %get-tuple-element.131) | copy-start | bytes 16
  19.6 18.3 %copy-start.139 = (pred[4]{0:T(512)(128)(4,1)}, pred[4]{0:T(512)(128)(4,1)S(1)}, u32[]{:S(2)}) copy-start(pred[4]{0:T(512)(128)(4,1)S(1)} %get-tuple-element.274) | copy-start | bytes 16
  19.6 18.3 %copy-start.140 = (pred[4]{0:T(512)(128)(4,1)}, pred[4]{0:T(512)(128)(4,1)S(1)}, u32[]{:S(2)}) copy-start(pred[4]{0:T(512)(128)(4,1)S(1)} %get-tuple-element.275) | copy-start | bytes 16
  19.6 18.3 %copy-start.141 = (pred[4]{0:T(512)(128)(4,1)}, pred[4]{0:T(512)(128)(4,1)S(1)}, u32[]{:S(2)}) copy-start(pred[4]{0:T(512)(128)(4,1)S(1)} %get-tuple-element.130) | copy-start | bytes 16
  19.6 18.3 %copy-start.143 = (pred[4]{0:T(512)(128)(4,1)}, pred[4]{0:T(512)(128)(4,1)S(1)}, u32[]{:S(2)}) copy-start(pred[4]{0:T(512)(128)(4,1)S(1)} %get-tuple-element.272) | copy-start | bytes 16
  19.6 18.3 %copy-start.145 = (pred[4]{0:T(512)(128)(4,1)}, pred[4]{0:T(512)(128)(4,1)S(1)}, u32[]{:S(2)}) copy-start(pred[4]{0:T(512)(128)(4,1)S(1)} %get-tuple-element.273) | copy-start | bytes 16
  19.6 18.3 %copy-start.147 = (pred[4]{0:T(512)(128)(4,1)}, pred[4]{0:T(512)(128)(4,1)S(1)}, u32[]{:S(2)}) copy-start(pred[4]{0:T(512)(128)(4,1)S(1)} %get-tuple-element.265) | copy-start | bytes 16
  19.6 18.3 %copy-start.148 = (pred[4]{0:T(512)(128)(4,1)}, pred[4]{0:T(512)(128)(4,1)S(1)}, u32[]{:S(2)}) copy-start(pred[4]{0:T(512)(128)(4,1)S(1)} %get-tuple-element.268) | copy-start | bytes 16
  19.6 18.3 %copy-start.149 = (pred[4]{0:T(512)(128)(4,1)}, pred[4]{0:T(512)(128)(4,1)S(1)}, u32[]{:S(2)}) copy-start(pred[4]{0:T(512)(128)(4,1)S(1)} %get-tuple-element.269) | copy-start | bytes 16
  19.6 18.3 %copy-start.150 = (pred[4]{0:T(512)(128)(4,1)}, pred[4]{0:T(512)(128)(4,1)S(1)}, u32[]{:S(2)}) copy-start(pred[4]{0:T(512)(128)(4,1)S(1)} %get-tuple-element.280) | copy-start | bytes 16
  19.6 18.3 %copy-start.151 = (pred[4]{0:T(512)(128)(4,1)}, pred[4]{0:T(512)(128)(4,1)S(1)}, u32[]{:S(2)}) copy-start(pred[4]{0:T(512)(128)(4,1)S(1)} %get-tuple-element.281) | copy-start | bytes 16
  19.7 18.3 %copy-start.152 = (pred[4]{0:T(512)(128)(4,1)}, pred[4]{0:T(512)(128)(4,1)S(1)}, u32[]{:S(2)}) copy-start(pred[4]{0:T(512)(128)(4,1)S(1)} %get-tuple-element.282) | copy-start | bytes 16
  61.2 20.7 %copy-start.32 = (f32[192]{0:T(256)S(1)}, f32[192]{0:T(256)}, u32[]{:S(2)}) copy-start(f32[192]{0:T(256)} %param.13) | copy-start | bytes 2308
  287.0 7.8 %collective-permute-start.2 = (bf16[4,4,3,16,192]{4,0,3,2,1:T(4,128)(2,1)}, bf16[4,4,3,16,192]{4,0,3,2,1:T(4,128)(2,1)S(1)}, u32[]{:S(2)}, u32[]{:S(2)}) collective-permute-start(bf16[4,4,3,16,192]{4,0,3,2,1:T(4,128)(2,1)} %get-tuple-element.163), channel_id=1, source_target_pairs={{0,31},{1,0},{2,1},{3,2},{4,3},{5,4},{6,5},{7,6},{8,7},{9,8},{10,9... | collective-permute-start | bytes 884744 | tf_op jit(solution)/shard_map/ppermute | solution.py:40
  287.9 6.9 %collective-permute-start.3 = (bf16[4,4,3,16,192]{4,0,3,2,1:T(4,128)(2,1)}, bf16[4,4,3,16,192]{4,0,3,2,1:T(4,128)(2,1)}, u32[]{:S(2)}, u32[]{:S(2)}) collective-permute-start(bf16[4,4,3,16,192]{4,0,3,2,1:T(4,128)(2,1)} %get-tuple-element.164), channel_id=1, source_target_pairs={{0,1},{1,2},{2,3},{3,4},{4,5},{5,6},{6,7},{7,8},{8,9},{9,10},{10,1... | collective-permute-start | bytes 884744 | tf_op jit(solution)/shard_map/ppermute | solution.py:40
  297.0 248.3 %copy-start.1 = (bf16[192,768]{1,0:T(8,128)(2,1)S(1)}, bf16[192,768]{1,0:T(8,128)(2,1)}, u32[]{:S(2)}) copy-start(bf16[192,768]{1,0:T(8,128)(2,1)} %param.15) | copy-start | bytes 884740
  (185 other events, 906.5 us)
Sparse Core Ops, SparseCore 0:
  289.5 251.9 all-reduce.24
where the time goes:
time: 562 us; the launch traced here: 552 us
  waiting for transfers between devices  246 us (44%)
  other arithmetic  130 us (23%)
  blocking collectives  84.3 us (15%)
  local copies, waits for them, and re-layouts  37.2 us (7%)
  matrix products  31.7 us (6%)
  between operations  18.1 us (3%)
    psum x1, waiting for transfers between devices, on_device(): lax.psum((grad_k, gain_gradient, grad_b, grad_up, grad_up_b, grad_down),...  243 us
    psum x1, blocking collectives, on_device(): lax.psum((grad_k, gain_gradient, grad_b, grad_up, grad_up_b, grad_down),...  84.3 us
    add x1, other arithmetic, on_device(): d_padded + depth_kernel[offset_row, offset_col] * spread[:, 6 - offset_ro...  46 us
    reduce_sum x4, other arithmetic, on_device(): jnp.sum(padded[:, offset_row:offset_row + tile_side, offset_col:offset_co...  21.7 us
    reduce_sum x1, other arithmetic, on_device(): average = jnp.mean(mixed, axis=-1, keepdims=True)  19.9 us
    dot_general x8, matrix products, on_device(): jnp.einsum('te,tabcd->eabcd', onehot, contribution, precision=lax.Precisi...  19.7 us
    convert_element_type x25, other arithmetic, slot_return(): (quarter_turns == quarter).astype(jnp.float32)[:, None, None, None, None]  13.9 us
  transfers between devices with their start and end apart: 5, of which 2 were waited for; matrix products, arithmetic and copies ran while one was open for 5% of the time, Pallas kernels for 0%

commit v1 on v0

v1 whole, which is shorter than its diff:
```python
import math

import jax
import jax.numpy as jnp
from jax import lax
from jax.experimental import pallas as pl
from jax.experimental.pallas import tpu as pltpu
from jax.sharding import Mesh, PartitionSpec as P

GELU_C = math.sqrt(2.0 / math.pi)
EPSILON = 1e-06
F32 = jnp.float32
BF16 = jnp.bfloat16
T = 4
S = 16
PX = S * S
C = 192
HID = 768
W = 24
DW = 32
WEIGHT_ROWS = 2 * C * HID // 128
ROWS = 2560


def gelu_pair(value):
    square = value * value
    tangent = jnp.tanh(GELU_C * (value + 0.044715 * square * value))
    half = 0.5 * (1.0 + tangent)
    result = value * half
    slope = half + 0.5 * value * (1.0 - tangent * tangent) * (GELU_C + GELU_C * 3.0 * 0.044715 * square)
    return (result, slope)


def turn_of(quarter):
    on_i = jnp.where(quarter == 0, S, jnp.where(quarter == 1, -1, jnp.where(quarter == 2, -S, 1)))
    on_j = jnp.where(quarter == 0, 1, jnp.where(quarter == 1, S, jnp.where(quarter == 2, -1, -S)))
    base = jnp.where(
        quarter == 0, 0, jnp.where(quarter == 1, S - 1, jnp.where(quarter == 2, PX - 1, PX - S))
    )
    return on_i, on_j, base


SLOTS = (
    (0, S - 3, -3, 3, 19),
    (2, 0, -3, 3, 19),
    (1, 0, S - 3, 0, 3),
    (1, 0, -19, 19, 22),
    (0, S - 3, S - 3, 0, 3),
    (0, S - 3, -19, 19, 22),
    (2, 0, S - 3, 0, 3),
    (2, 0, -19, 19, 22),
)
FIRST = (0, 3, 19)
COUNT = (3, S, 3)


def slot_match(slot, quarter, transposed):
    group, row0, col0, low, high = SLOTS[slot]
    length = COUNT[group] * W
    shape = (PX, length) if transposed else (length, PX)
    along = 1 if transposed else 0
    line = (1, length) if transposed else (length, 1)
    place = lax.broadcasted_iota(jnp.int32, line, along)
    row = place // W
    col = place - row * W
    on_i, on_j, base = turn_of(quarter)
    source = on_i * (row + row0) + on_j * (col + col0) + base
    source = jnp.where((col >= low) & (col < high), source, -1)
    return (lax.broadcasted_iota(jnp.int32, shape, 1 - along) == source).astype(F32).astype(BF16)


def block_kernel(
    pos_ref,
    turn_ref,
    prev_ref,
    own_ref,
    next_ref,
    cot_ref,
    cot_t_ref,
    kern_ref,
    gain_ref,
    bias_ref,
    up_ref,
    up_bias_ref,
    down_t_ref,
    down_ref,
    up_t_ref,
    updated_ref,
    part_ref,
    to_prev_ref,
    to_next_ref,
    grads_ref,
    src,
    pad,
    mix,
    xhat,
    inv,
    normed,
    dmix,
    dpad,
    collected,
    g_up,
    g_down_t,
    g_up_bias,
    g_small,
):
    lane = lax.broadcasted_iota(jnp.int32, (1, 128), 1)
    low_half = lane < 64

    src[:, :, 128:] = jnp.zeros((3 * T, PX, 128), BF16)
    src[0:T, :, :C] = prev_ref[...]
    src[T : 2 * T, :, :C] = own_ref[...]
    src[2 * T :, :, :C] = next_ref[...]
    g_up[...] = jnp.zeros_like(g_up)
    g_down_t[...] = jnp.zeros_like(g_down_t)
    g_up_bias[...] = jnp.zeros_like(g_up_bias)
    g_small[...] = jnp.zeros_like(g_small)
    dmix[...] = jnp.zeros_like(dmix)
    collected[...] = jnp.zeros_like(collected)

    @pl.loop(0, T // 2)
    def _(pair):
        for half in range(2):
            tile = pair * 2 + half
            for group in range(3):
                total = None
                for slot in range(8):
                    if SLOTS[slot][0] != group:
                        continue
                    match = slot_match(slot, turn_ref[tile * 8 + slot], False)
                    piece = jnp.dot(
                        match, src[pos_ref[tile * 8 + slot]], preferred_element_type=F32
                    )
                    total = piece if total is None else total + piece
                if group == 1:
                    place = lax.broadcasted_iota(jnp.int32, (S * W, 1), 0)
                    row = place // W
                    col = place - row * W - 3
                    source = jnp.where((col >= 0) & (col < S), row * S + col, -1)
                    match = lax.broadcasted_iota(jnp.int32, (S * W, PX), 1) == source
                    total = total + jnp.dot(
                        match.astype(F32).astype(BF16), src[T + tile], preferred_element_type=F32
                    )
                rows = pl.ds(FIRST[group] * W, COUNT[group] * W)
                if half == 0:
                    pad[pair * 3, rows, :] = total[:, :128]
                    pad[pair * 3 + 1, rows, :] = total[:, 128:]
                else:
                    total = pltpu.roll(total, 64, 1)
                    pad[pair * 3 + 1, rows, :] += total[:, :128]
                    pad[pair * 3 + 2, rows, :] = total[:, 128:]

    @pl.loop(0, 3 * T // 2)
    def _(slab):
        part = lax.rem(slab, 3)
        for half in range(2):
            acc = [None] * S
            for b in range(7):
                taps = [kern_ref[part, a * 7 + b : a * 7 + b + 1, :] for a in range(7)]
                for m in range(S + 6):
                    x = pad[slab, pl.ds(m * W + b + 8 * half, 8), :]
                    for a in range(7):
                        i = m - a
                        if 0 <= i < S:
                            term = x * taps[a]
                            acc[i] = term if acc[i] is None else acc[i] + term
            for i in range(S):
                mix[slab, pl.ds(i * S + 8 * half, 8), :] = acc[i]

    def pair_means(s0, s1, s2):
        first = jnp.sum(s0 + jnp.where(low_half, s1, 0.0), axis=1, keepdims=True) * (1.0 / C)
        second = jnp.sum(s2 + jnp.where(low_half, 0.0, s1), axis=1, keepdims=True) * (1.0 / C)
        return first, jnp.where(low_half, first, second), second

    CH = 64

    @pl.loop(0, (T // 2) * (PX // CH))
    def _(step):
        pair = step // (PX // CH)
        rows = pl.ds(pl.multiple_of(lax.rem(step, PX // CH) * CH, CH), CH)
        slabs = [mix[pair * 3 + k, rows, :] for k in range(3)]
        means = pair_means(*slabs)
        slabs = [x - m for x, m in zip(slabs, means)]
        spreads = pair_means(*[x * x for x in slabs])
        for k in range(3):
            deviation = jnp.broadcast_to(lax.rsqrt(spreads[k] + EPSILON), (CH, 128))
            standard = slabs[k] * deviation
            inv[pair * 3 + k, rows, :] = deviation
            xhat[pair * 3 + k, rows, :] = standard
            normed[pair, rows, 128 * k : 128 * (k + 1)] = (
                standard * gain_ref[k] + bias_ref[k]
            ).astype(BF16)

    @pl.loop(0, T // 2)
    def _(pair):
        normed_grads = []
        for half in range(2):
            tile = pair * 2 + half
            x = normed[pair, :, 128 * half : 128 * half + 256]
            x_t = jnp.transpose(x.astype(F32)).astype(BF16)
            cot = cot_ref[tile]
            cot_t = cot_t_ref[tile]
            branch = jnp.zeros((PX, C), F32)
            normed_grad = jnp.zeros((PX, 256), F32)
            for chunk in range(3):
                hid = slice(256 * chunk, 256 * (chunk + 1))
                up_value = (
                    jnp.dot(x, up_ref[half, :, hid], preferred_element_type=F32)
                    + up_bias_ref[:, hid]
                )
                value, slope = gelu_pair(up_value)
                activation = value.astype(BF16)
                branch += jnp.dot(activation, down_ref[hid, :], preferred_element_type=F32)
                d_up = jnp.dot(cot, down_t_ref[:, hid], preferred_element_type=F32) * slope
                g_up_bias[:, hid] += jnp.sum(d_up.reshape(PX // 8, 8, 256), axis=0)
                d_up_b = d_up.astype(BF16)
                g_down_t[:, hid] += jnp.dot(cot_t, activation, preferred_element_type=F32)
                up_grad = jnp.dot(x_t, d_up_b, preferred_element_type=F32)
                g_up[:, hid] += up_grad[64 * half : 64 * half + C]
                normed_grad += jnp.dot(d_up_b, up_t_ref[half, hid, :], preferred_element_type=F32)
            updated_ref[tile] = (own_ref[tile].astype(F32) + branch).astype(BF16)
            normed_grads.append(normed_grad)
        mix[pair * 3] = normed_grads[0][:, :128]
        mix[pair * 3 + 1] = normed_grads[0][:, 128:] + normed_grads[1][:, :128]
        mix[pair * 3 + 2] = normed_grads[1][:, 128:]

    @pl.loop(0, (T // 2) * (PX // CH))
    def _(step):
        pair = step // (PX // CH)
        start = pl.multiple_of(lax.rem(step, PX // CH) * CH, CH)
        rows = pl.ds(start, CH)
        grads = [mix[pair * 3 + k, rows, :] for k in range(3)]
        standard = [xhat[pair * 3 + k, rows, :] for k in range(3)]
        for k in range(3):
            g_small[k, 8 * 49 : 8 * 50, :] += jnp.sum(
                (grads[k] * standard[k]).reshape(CH // 8, 8, 128), axis=0
            )
            g_small[k, 8 * 50 : 8 * 51, :] += jnp.sum(grads[k].reshape(CH // 8, 8, 128), axis=0)
        scaled = [grads[k] * gain_ref[k] for k in range(3)]
        means = pair_means(*scaled)
        products = pair_means(*[e * x for e, x in zip(scaled, standard)])
        for k in range(3):
            d_mixed = inv[pair * 3 + k, rows, :] * (
                scaled[k] - means[k] - standard[k] * products[k]
            )
            for r in range(CH // S):
                at = (start // S + r) * DW + 8
                dmix[pair * 3 + k, pl.ds(pl.multiple_of(at, 8), S), :] = d_mixed[r * S : (r + 1) * S]

    @pl.loop(0, 3 * T // 2)
    def _(slab):
        part = lax.rem(slab, 3)
        for half in range(2):
            grads = [dmix[slab, pl.ds(i * DW + 8 + 8 * half, 8), :] for i in range(S)]
            for b in range(7):
                acc = [None] * 7
                for m in range(S + 6):
                    x = pad[slab, pl.ds(m * W + b + 8 * half, 8), :]
                    for a in range(7):
                        i = m - a
                        if 0 <= i < S:
                            term = x * grads[i]
                            acc[a] = term if acc[a] is None else acc[a] + term
                for a in range(7):
                    g_small[part, 8 * (a * 7 + b) : 8 * (a * 7 + b + 1), :] += acc[a]
        for third in range(3):
            acc = [None] * (S + 6)
            for b in range(7):
                taps = [kern_ref[part, a * 7 + b : a * 7 + b + 1, :] for a in range(7)]
                for i in range(S):
                    x = dmix[slab, pl.ds(i * DW + 8 + 8 * third - b, 8), :]
                    for a in range(7):
                        term = x * taps[a]
                        acc[i + a] = term if acc[i + a] is None else acc[i + a] + term
            for m in range(S + 6):
                dpad[slab, pl.ds(m * W + 8 * third, 8), :] = acc[m]

    @pl.loop(0, T // 2)
    def _(pair):
        for half in range(2):
            tile = pair * 2 + half
            for slot in range(8):
                group = SLOTS[slot][0]
                rows = pl.ds(FIRST[group] * W, COUNT[group] * W)
                border = jnp.concatenate(
                    [dpad[pair * 3 + half + k, rows, :] for k in range(2)], axis=1
                ).astype(BF16)
                match = slot_match(slot, turn_ref[tile * 8 + slot], True)
                piece = jnp.dot(match, border, preferred_element_type=F32)
                if half == 1:
                    piece = pltpu.roll(piece, 192, 1)
                collected[pos_ref[tile * 8 + slot]] += piece

    to_prev_ref[...] = collected[0:T, :, :C].astype(BF16)
    to_next_ref[...] = collected[2 * T :, :, :C].astype(BF16)

    @pl.loop(0, T // 2)
    def _(pair):
        for half in range(2):
            tile = pair * 2 + half
            for i in range(S):
                rows = slice(i * S, (i + 1) * S)
                centre = jnp.concatenate(
                    [dpad[pair * 3 + half + k, pl.ds((i + 3) * W + 3, S), :] for k in range(2)],
                    axis=1,
                )
                if half == 1:
                    centre = pltpu.roll(centre, 192, 1)
                part_ref[tile, rows, :] = (
                    cot_ref[tile, rows, :].astype(F32)
                    + centre[:, :C]
                    + collected[T + tile, rows, :C]
                )

    for k in range(HID // 128):
        lanes = slice(128 * k, 128 * (k + 1))
        grads_ref[C * k : C * (k + 1), :] = g_up[:, lanes].astype(BF16)
        grads_ref[WEIGHT_ROWS // 2 + C * k : WEIGHT_ROWS // 2 + C * (k + 1), :] = g_down_t[
            :, lanes
        ].astype(BF16)
    sums = [jnp.sum(g_small[k].reshape(56, 8, 128), axis=1) for k in range(3)]
    crossed = pltpu.roll(jnp.where(low_half, sums[2], sums[1]), 64, 1)
    grads_ref[WEIGHT_ROWS : WEIGHT_ROWS + 56, :] = (sums[0] + crossed).astype(BF16)
    grads_ref[WEIGHT_ROWS + 56 : WEIGHT_ROWS + 112, :] = (
        sums[1] + pltpu.roll(sums[2], 64, 1)
    ).astype(BF16)
    bias_sum = jnp.sum(g_up_bias[...], axis=0, keepdims=True)
    bias_rows = jnp.concatenate(
        [bias_sum[:, 128 * k : 128 * (k + 1)] for k in range(6)] + [jnp.zeros((10, 128), F32)],
        axis=0,
    )
    grads_ref[WEIGHT_ROWS + 112 : WEIGHT_ROWS + 128, :] = bias_rows.astype(BF16)
    grads_ref[WEIGHT_ROWS + 128 :, :] = jnp.zeros((ROWS - WEIGHT_ROWS - 128, 128), BF16)


def run_block(pos, turns, prev, own, nxt, cot, cot_t, kern, gain, bias, up, up_bias, down_t, down, up_t):
    vmem = pl.BlockSpec(memory_space=pltpu.VMEM)
    smem = pl.BlockSpec(memory_space=pltpu.SMEM)
    slabs = 3 * T // 2
    tile = (T, PX, C)
    return pl.pallas_call(
        block_kernel,
        out_shape=(
            jax.ShapeDtypeStruct(tile, BF16),
            jax.ShapeDtypeStruct(tile, F32),
            jax.ShapeDtypeStruct(tile, BF16),
            jax.ShapeDtypeStruct(tile, BF16),
            jax.ShapeDtypeStruct((ROWS, 128), BF16),
        ),
        in_specs=[smem, smem] + [vmem] * 13,
        out_specs=(vmem,) * 5,
        scratch_shapes=[
            pltpu.VMEM((3 * T, PX, 256), BF16),
            pltpu.VMEM((slabs, 22 * W, 128), F32),
            pltpu.VMEM((slabs, PX, 128), F32),
            pltpu.VMEM((slabs, PX, 128), F32),
            pltpu.VMEM((slabs, PX, 128), F32),
            pltpu.VMEM((T // 2, PX, 384), BF16),
            pltpu.VMEM((slabs, S * DW, 128), F32),
            pltpu.VMEM((slabs, 22 * W, 128), F32),
            pltpu.VMEM((3 * T, PX, 256), F32),
            pltpu.VMEM((C, HID), F32),
            pltpu.VMEM((C, HID), F32),
            pltpu.VMEM((8, HID), F32),
            pltpu.VMEM((3, 8 * 56, 128), F32),
        ],
        compiler_params=pltpu.CompilerParams(vmem_limit_bytes=48 * 1024 * 1024),
        cost_estimate=pl.CostEstimate(flops=4 * 10**9, bytes_accessed=8 * 10**6, transcendentals=10**6),
    )(pos, turns, prev, own, nxt, cot, cot_t, kern, gain, bias, up, up_bias, down_t, down, up_t)


FLAT = ("y", "xl", "xh", "z")


def shared_with(x, axes, count):
    return lax.all_to_all(jnp.broadcast_to(x[None], (count,) + x.shape), axes, 0, 0)


def total_of(x):
    return jnp.sum(x.astype(F32), axis=0)


def sum_everywhere(grads):
    core = lax.axis_index("c")
    swap = [(0, 1), (1, 0)]
    halves = grads.reshape(2, ROWS // 2, 128)
    other = lax.ppermute(lax.dynamic_index_in_dim(halves, 1 - core, 0, keepdims=False), "c", swap)
    mine = lax.dynamic_index_in_dim(halves, core, 0, keepdims=False)
    mine = (mine.astype(F32) + other.astype(F32)).astype(BF16)
    plane = ("y", "xl", "xh")
    mine = total_of(lax.all_to_all(mine.reshape(16, ROWS // 32, 128), plane, 0, 0))
    mine = total_of(shared_with(mine.astype(BF16), "z", 8))
    mine = shared_with(mine.astype(BF16), plane, 16).reshape(ROWS // 2, 128)
    other = lax.ppermute(mine, "c", swap)
    return jnp.concatenate([jnp.where(core == 0, mine, other), jnp.where(core == 0, other, mine)])


def on_device(
    fields,
    depth_kernel,
    layer_norm_gain,
    layer_norm_bias,
    up_weight,
    up_bias,
    down_weight,
    cotangent,
    neighbours,
    rotation,
    tile_owner,
):
    around = ("xh", "z", "c")
    blocks = 32
    position = lax.axis_index(around)
    to_right = [(i, (i + 1) % blocks) for i in range(blocks)]
    to_left = [((i + 1) % blocks, i) for i in range(blocks)]
    own = fields.reshape(T, PX, C)
    cot = cotangent.reshape(T, PX, C)
    prev = lax.ppermute(own, around, to_right)
    nxt = lax.ppermute(own, around, to_left)

    every = jnp.arange(128, dtype=jnp.int32)
    own_rows = position * T + jnp.arange(T, dtype=jnp.int32)
    is_own = (tile_owner[None, :] == own_rows[:, None]).astype(jnp.int32)
    near_ids = jnp.sum(is_own[:, :, None] * neighbours[None], axis=1)
    turns = jnp.sum(is_own[:, :, None] * rotation[None], axis=1)
    near_rows = jnp.sum((near_ids[:, :, None] == every) * tile_owner, axis=2)
    pos = (near_rows // T - position + 1) % blocks * T + near_rows % T

    def packed(x):
        return jnp.concatenate([x, x], axis=-1).reshape(x.shape[:-1] + (3, 128))

    kern = jnp.transpose(packed(depth_kernel.reshape(49, C)), (1, 0, 2))
    kern = jnp.pad(kern, ((0, 0), (0, 7), (0, 0)))
    gain = packed(layer_norm_gain)[:, None, :]
    bias = packed(layer_norm_bias)[:, None, :]
    up = jnp.stack(
        [jnp.pad(up_weight, ((0, 64), (0, 0))), jnp.pad(up_weight, ((64, 0), (0, 0)))]
    )
    up_t = jnp.transpose(up, (0, 2, 1))
    updated, part, to_prev, to_next, grads = run_block(
        pos.reshape(-1),
        turns.reshape(-1),
        prev,
        own,
        nxt,
        cot,
        jnp.transpose(cot, (0, 2, 1)),
        kern,
        gain,
        bias,
        up,
        up_bias[None],
        down_weight.T,
        down_weight,
        up_t,
    )
    from_right = lax.ppermute(to_prev, around, to_left)
    from_left = lax.ppermute(to_next, around, to_right)
    sums = sum_everywhere(grads)
    grad_fields = (part + from_right.astype(F32) + from_left.astype(F32)).astype(BF16)

    scale = 1.0 / math.sqrt(8 * blocks * T * PX)
    sums = sums.astype(F32) * scale
    half = WEIGHT_ROWS // 2
    grad_up = jnp.concatenate([sums[C * k : C * (k + 1)] for k in range(6)], axis=1)
    grad_down = jnp.concatenate(
        [sums[half + C * k : half + C * (k + 1)].T for k in range(6)], axis=0
    )
    small = jnp.concatenate(
        [sums[WEIGHT_ROWS : WEIGHT_ROWS + 56], sums[WEIGHT_ROWS + 56 : WEIGHT_ROWS + 112, :64]],
        axis=1,
    )
    return (
        updated.reshape(fields.shape),
        grad_fields.reshape(fields.shape),
        small[:49].reshape(7, 7, C),
        small[49],
        small[50],
        grad_up,
        sums[WEIGHT_ROWS + 112 : WEIGHT_ROWS + 118].reshape(-1),
        grad_down,
    )


def solution(mesh):
    fine = Mesh(mesh.devices.reshape(4, 2, 2, 8, 2), ("y", "xl", "xh", "z", "c"))
    tiles = P(("y", "xl"), ("xh", "z", "c"), None, None, None)
    return jax.shard_map(
        on_device,
        mesh=fine,
        in_specs=(tiles, P(), P(), P(), P(), P(), P(), tiles, P(), P(), P()),
        out_specs=(tiles, tiles, P(), P(), P(), P(), P(), P()),
        check_vma=False,
    )
```

time: 562 us -> 96.5 us (0.17); the launches traced: 552 us -> 96 us
  waiting for transfers between devices: 246 us -> 6.71 us
  other arithmetic: 130 us -> 6.71 us
  blocking collectives: 84.3 us -> 23.8 us
  matrix products: 31.7 us -> 0 us
  local copies, waits for them, and re-layouts: 37.2 us -> 9.87 us
  Pallas kernels: 0 us -> 24.7 us
  starting transfers between devices: 5.1 us -> 23.2 us
  between operations: 18.1 us -> 0.96 us
    psum x1 -> x0, waiting for transfers between devices: 243 us -> none  [on_device(): lax.psum((grad_k, gain_gradient, grad_b, grad_up, grad_up_b, grad_down),...]
    psum x1 -> x0, blocking collectives: 84.3 us -> none  [on_device(): lax.psum((grad_k, gain_gradient, grad_b, grad_up, grad_up_b, grad_down),...]
    add x3 -> x2, other arithmetic: 47.9 us -> 0.03 us  [the longest x1 0.02 us: on_device(): pos = (near_rows // T - position + 1) % blocks * T + near_rows % T]
    reduce_sum x7 -> x4, other arithmetic: 45 us -> 1.87 us  [the longest x1 0.92 us: on_device(): turns = jnp.sum(is_own[:, :, None] * rotation[None], axis=1)]
    dot_general x14 -> x0, matrix products: 31.7 us -> none  [the longest x8 19.7 us: on_device(): jnp.einsum('te,tabcd->eabcd', onehot, contribution, precision=lax.Precisi...]
    pallas_call x0 -> x1, Pallas kernels: none -> 24.7 us  [run_block(): pl.pallas_call(block_kernel, out_shape=(jax.ShapeDtypeStruct(tile, BF16),...]
    all_to_all x0 -> x2, blocking collectives: none -> 23.8 us  [the longest x1 12.5 us: sum_everywhere(): lax.all_to_all(mine.reshape(16, ROWS // 32, 128), plane, 0, 0)]
    convert_element_type x27 -> x3, other arithmetic: 17.5 us -> 2.81 us  [the longest x1 2 us: on_device(): (part + from_right.astype(F32) + from_left.astype(F32)).astype(BF16)]
  transfers between devices with their start and end apart: 5 -> 7, of which waited for: 2 -> 3; matrix products, arithmetic and copies ran while one was open for 5% -> 8% of each run, Pallas kernels for 0% -> 0%
where the time goes in v1:
time: 96.5 us; the launch traced here: 96 us
  Pallas kernels  24.7 us (26%)
  blocking collectives  23.8 us (25%)
  starting transfers between devices  23.2 us (24%)
  local copies, waits for them, and re-layouts  9.87 us (10%)
  other arithmetic  6.71 us (7%)
  waiting for transfers between devices  6.71 us (7%)
    pallas_call x1, Pallas kernels, run_block(): pl.pallas_call(block_kernel, out_shape=(jax.ShapeDtypeStruct(tile, BF16),...  24.7 us
    all_to_all x1, blocking collectives, sum_everywhere(): lax.all_to_all(mine.reshape(16, ROWS // 32, 128), plane, 0, 0)  12.5 us
    all_to_all x1, blocking collectives, shared_with(): lax.all_to_all(jnp.broadcast_to(x[None], (count,) + x.shape), axes, 0, 0)  11.3 us
    unnamed x44, local copies, waits for them, and re-layouts  6.78 us
    all_to_all x1, starting transfers between devices, shared_with(): lax.all_to_all(jnp.broadcast_to(x[None], (count,) + x.shape), axes, 0, 0)  5.67 us
    ppermute x1, starting transfers between devices, sum_everywhere(): lax.ppermute(lax.dynamic_index_in_dim(halves, 1 - core, 0, keepdims=False...  5.08 us
    ppermute x1, starting transfers between devices, sum_everywhere(): other = lax.ppermute(mine, 'c', swap)  5.03 us
    all_to_all x1, waiting for transfers between devices, shared_with(): lax.all_to_all(jnp.broadcast_to(x[None], (count,) + x.shape), axes, 0, 0)  4.38 us
  transfers between devices with their start and end apart: 7, of which 3 were waited for; matrix products, arithmetic and copies ran while one was open for 8% of the time, Pallas kernels for 0%

profile of v1, /device:TPU:1, one launch (start us, length us, event | category | flops | bytes accessed | tf_op | source)
XLA Modules:
  0.0 96.0 jit_solution(6167830399639874550)
XLA Ops:
  0.6 3.1 %collective-permute-start = (bf16[4,256,192]{2,1,0:T(8,128)(2,1)}, bf16[4,256,192]{2,1,0:T(8,128)(2,1)S(1)}, u32[]{:S(2)}, u32[]{:S(2)}) collective-permute-start(bf16[4,256,192]{2,1,0:T(8,128)(2,1)} %bitcast.59), channel_id=1, source_target_pairs={{0,1},{1,2},{2,3},{3,4},{4,5},{5,6},{6,7},{7,8},{8,9},{9,10},{10,1... | collective-permute-start | bytes 1179656 | tf_op jit(solution)/shard_map/ppermute | solution.py:418
  4.0 0.7 compare_convert_fusion
  4.8 0.9 multiply_reduce_fusion
  5.7 0.9 select_reduce_fusion
  6.7 1.1 %copy.37 = bf16[192,768]{0,1:T(8,128)(2,1)S(1)} copy(bf16[192,768]{1,0:T(8,128)(2,1)} %param.15) | data formatting | bytes 589824 | tf_op args[4]
  8.1 1.0 %fusion.12 = (bf16[2,768,256]{2,1,0:T(8,128)(2,1)}, bf16[2,256,768]{1,2,0:T(8,128)(2,1)S(1)}) fusion(bf16[1,256,768]{1,2,0:T(8,128)(2,1)S(1)} %get-tuple-element.25, bf16[1,256,768]{1,2,0:T(8,128)(2,1)S(1)} %get-tuple-element.24), kind=kLoop, calls=%fused_computation.57 | loop fusion | flops 393216 | bytes 2359296 | tf_op jit(solution)/shard_map/transpose | solution.py:439
  11.0 0.8 copy-done.3
  11.8 1.1 %collective-permute-done.1.next_ref = bf16[4,256,192]{2,1,0:T(8,128)(2,1)} collective-permute-done((bf16[4,256,192]{2,1,0:T(8,128)(2,1)}, bf16[4,256,192]{2,1,0:T(8,128)(2,1)}, u32[]{:S(2)}, u32[]{:S(2)}) %collective-permute-start.1) | collective-permute-done | bytes 393248 | tf_op jit(solution)/shard_map/ppermute | solution.py:419
  12.9 1.0 %copy-done.2 = bf16[1,4,16,16,192]{4,3,2,1,0:T(8,128)(2,1)S(1)} copy-done((bf16[1,4,16,16,192]{4,3,2,1,0:T(8,128)(2,1)S(1)}, bf16[1,4,16,16,192]{4,3,2,1,0:T(8,128)(2,1)}, u32[]{:S(2)}) %copy-start.2) | copy-done | bytes 393240
  13.9 1.0 %copy-done.4 = bf16[4,256,192]{2,1,0:T(8,128)(2,1)S(1)} copy-done((bf16[4,256,192]{2,1,0:T(8,128)(2,1)S(1)}, bf16[4,256,192]{2,1,0:T(8,128)(2,1)}, u32[]{:S(2)}) %copy-start.4) | copy-done | bytes 393240
  14.9 24.7 %shard_map.170 = (bf16[4,256,192]{2,1,0:T(8,128)(2,1)}, f32[4,256,192]{2,1,0:T(8,128)}, bf16[4,256,192]{2,1,0:T(8,128)(2,1)S(1)}, bf16[4,256,192]{2,1,0:T(8,128)(2,1)S(1)}, bf16[2560,128]{1,0:T(8,128)(2,1)S(1)}) custom-call(s32[32]{0:T(128)S(1)} %fusion.9.pos_ref, s32[32]{0:T(128)S(1)} %reshape.93.turn_ref, bf16[4,256,192]{2,1,0:T(8,128)(2,1)S(1)} %copy-done.4, ...), custom_call_target="tpu_custom_call" | custom-call | flops 4000000000 | bytes 8000000 | tf_op jit(solution)/shard_map/pallas_call | solution.py:341
  39.7 0.8 copy-done.5
  40.5 0.8 copy-done.7
  41.3 5.1 %collective-permute-start.4 = (bf16[1280,128]{1,0:T(8,128)(2,1)S(1)}, bf16[1280,128]{1,0:T(8,128)(2,1)S(1)}, u32[]{:S(2)}, u32[]{:S(2)}) collective-permute-start(bf16[1280,128]{1,0:T(8,128)(2,1)S(1)} %dynamic-slice_bitcast_fusion), channel_id=1, source_target_pairs={{0,1},{1,0},{2,3},{3,2},{4,5},{5,4},{6,7},{7,6},{8,9},{9,8},{10,11... | collective-permute-start | bytes 983048 | tf_op jit(solution)/shard_map/ppermute | solution.py:387
  46.4 1.3 %collective-permute-done.4 = bf16[1280,128]{1,0:T(8,128)(2,1)S(1)} collective-permute-done((bf16[1280,128]{1,0:T(8,128)(2,1)S(1)}, bf16[1280,128]{1,0:T(8,128)(2,1)S(1)}, u32[]{:S(2)}, u32[]{:S(2)}) %collective-permute-start.4) | collective-permute-done | bytes 327712 | tf_op jit(solution)/shard_map/ppermute | solution.py:387
  47.7 12.5 %all_to_all.15 = bf16[16,80,128]{2,1,0:T(8,128)(2,1)S(1)} all-to-all(bf16[16,80,128]{2,1,0:T(8,128)(2,1)S(1)} %bitcast.62), channel_id=1, replica_groups=mesh['y'=4,'xl'=2,'xh'=2,'z'=8,'c'=2] {'y','xl','xh'}, dimensions={0} | all-to-all | bytes 655360 | tf_op jit(solution)/shard_map/all_to_all | solution.py:391
  61.0 5.7 %all-to-all-start.1 = ((bf16[8,80,128]{2,1,0:T(8,128)(2,1)}), bf16[8,80,128]{2,1,0:T(8,128)(2,1)S(1)}, u32[]{:S(2)}, u32[]{:S(2)}) async-start(bf16[8,80,128]{2,1,0:T(8,128)(2,1)} %broadcast_in_dim.7), calls=%async_computation.1 | async-start | bytes 327680 | tf_op jit(solution)/shard_map/all_to_all | solution.py:376
  66.7 2.4 %collective-permute-start.2 = (bf16[4,256,192]{2,1,0:T(8,128)(2,1)S(1)}, bf16[4,256,192]{2,1,0:T(8,128)(2,1)S(1)}, u32[]{:S(2)}, u32[]{:S(2)}) collective-permute-start(bf16[4,256,192]{2,1,0:T(8,128)(2,1)S(1)} %copy-done.8), channel_id=1, source_target_pairs={{1,0},{2,1},{3,2},{4,3},{5,4},{6,5},{7,6},{8,7},{9,8},{10,9},{11,1... | collective-permute-start | bytes 1179656 | tf_op jit(solution)/shard_map/ppermute | solution.py:457
  69.0 1.6 %collective-permute-start.3 = (bf16[4,256,192]{2,1,0:T(8,128)(2,1)S(1)}, bf16[4,256,192]{2,1,0:T(8,128)(2,1)}, u32[]{:S(2)}, u32[]{:S(2)}) collective-permute-start(bf16[4,256,192]{2,1,0:T(8,128)(2,1)S(1)} %copy-done.6), channel_id=1, source_target_pairs={{0,1},{1,2},{2,3},{3,4},{4,5},{5,6},{6,7},{7,8},{8,9},{9,10},{10,1... | collective-permute-start | bytes 1179656 | tf_op jit(solution)/shard_map/ppermute | solution.py:458
  70.7 4.4 %all-to-all-done.1 = bf16[8,80,128]{2,1,0:T(8,128)(2,1)S(1)} async-done(((bf16[8,80,128]{2,1,0:T(8,128)(2,1)}), bf16[8,80,128]{2,1,0:T(8,128)(2,1)S(1)}, u32[]{:S(2)}, u32[]{:S(2)}) %all-to-all-start.1) | async-done | bytes 163872 | tf_op jit(solution)/shard_map/all_to_all | solution.py:376
  75.1 11.3 %all_to_all.16 = bf16[16,80,128]{2,1,0:T(8,128)(2,1)S(1)} all-to-all(bf16[16,80,128]{2,1,0:T(8,128)(2,1)S(1)} %broadcast_in_dim.8), channel_id=1, replica_groups=mesh['y'=4,'xl'=2,'xh'=2,'z'=8,'c'=2] {'y','xl','xh'}, dimensions={0} | all-to-all | bytes 655360 | tf_op jit(solution)/shard_map/all_to_all | solution.py:376
  86.4 5.0 %collective-permute-start.5 = (bf16[1280,128]{1,0:T(8,128)(2,1)S(1)}, bf16[1280,128]{1,0:T(8,128)(2,1)S(1)}, u32[]{:S(2)}, u32[]{:S(2)}) collective-permute-start(bf16[1280,128]{1,0:T(8,128)(2,1)S(1)} %bitcast.63), channel_id=1, source_target_pairs={{0,1},{1,0},{2,3},{3,2},{4,5},{5,4},{6,7},{7,6},{8,9},{9,8},{10,11... | collective-permute-start | bytes 983048 | tf_op jit(solution)/shard_map/ppermute | solution.py:394
  91.4 2.0 %add_convert_fusion = bf16[4,256,192]{2,1,0:T(8,128)(2,1)} fusion(bf16[4,256,192]{2,1,0:T(8,128)(2,1)} %collective-permute-done.3, f32[4,256,192]{2,1,0:T(8,128)S(1)} %copy-done.9, bf16[4,256,192]{2,1,0:T(8,128)(2,1)S(1)} %collective-permute-done.2), kind=kLoop, calls=%fused_computation.1 | loop fusion | flops 983040 | bytes 1966080 | tf_op jit(solution)/shard_map/convert_element_type | solution.py:460
  95.0 0.8 reshape.103
  (75 shorter events, 5.0 us)
Async XLA Ops:
  0.6 10.3 %collective-permute-start = (bf16[4,256,192]{2,1,0:T(8,128)(2,1)}, bf16[4,256,192]{2,1,0:T(8,128)(2,1)S(1)}, u32[]{:S(2)}, u32[]{:S(2)}) collective-permute-start(bf16[4,256,192]{2,1,0:T(8,128)(2,1)} %bitcast.59), channel_id=1, source_target_pairs={{0,1},{1,2},{2,3},{3,4},{4,5},{5,6},{6,7},{7,8},{8,9},{9,10},{10,1... | collective-permute-start | bytes 1179656 | tf_op jit(solution)/shard_map/ppermute | solution.py:418
  3.7 9.1 %collective-permute-start.1 = (bf16[4,256,192]{2,1,0:T(8,128)(2,1)}, bf16[4,256,192]{2,1,0:T(8,128)(2,1)}, u32[]{:S(2)}, u32[]{:S(2)}) collective-permute-start(bf16[4,256,192]{2,1,0:T(8,128)(2,1)} %bitcast.60), channel_id=1, source_target_pairs={{1,0},{2,1},{3,2},{4,3},{5,4},{6,5},{7,6},{8,7},{9,8},{10,9},{11,1... | collective-permute-start | bytes 1179656 | tf_op jit(solution)/shard_map/ppermute | solution.py:419
  9.1 1.0 %copy-start = (bf16[1,4,16,16,192]{4,3,2,1,0:T(8,128)(2,1)S(1)}, bf16[1,4,16,16,192]{4,3,2,1,0:T(8,128)(2,1)}, u32[]{:S(2)}) copy-start(bf16[1,4,16,16,192]{4,3,2,1,0:T(8,128)(2,1)} %param.18) | copy-start | bytes 1179652
  9.1 1.2 %copy-start.10 = (f32[7,7,192]{2,1,0:T(8,128)S(1)}, f32[7,7,192]{2,1,0:T(8,128)}, u32[]{:S(2)}) copy-start(f32[7,7,192]{2,1,0:T(8,128)} %param.12) | copy-start | bytes 112900
  9.1 1.4 %copy-start.1 = (bf16[768,192]{0,1:T(8,128)(2,1)S(1)}, bf16[768,192]{0,1:T(8,128)(2,1)}, u32[]{:S(2)}) copy-start(bf16[768,192]{0,1:T(8,128)(2,1)} %param.17) | copy-start | bytes 884740
  9.4 1.3 %copy-start.14 = (f32[192]{0:T(256)S(1)}, f32[192]{0:T(256)}, u32[]{:S(2)}) copy-start(f32[192]{0:T(256)} %param.13) | copy-start | bytes 2308
  9.4 1.4 %copy-start.15 = (f32[192]{0:T(256)S(1)}, f32[192]{0:T(256)}, u32[]{:S(2)}) copy-start(f32[192]{0:T(256)} %param.14) | copy-start | bytes 2308
  9.4 1.5 %copy-start.13 = (f32[768]{0:T(1024)S(1)}, f32[768]{0:T(1024)}, u32[]{:S(2)}) copy-start(f32[768]{0:T(1024)} %param.16) | copy-start | bytes 9220
  11.0 0.8 copy-start.3
  12.8 1.0 %copy-start.2 = (bf16[1,4,16,16,192]{4,3,2,1,0:T(8,128)(2,1)S(1)}, bf16[1,4,16,16,192]{4,3,2,1,0:T(8,128)(2,1)}, u32[]{:S(2)}) copy-start(bf16[1,4,16,16,192]{4,3,2,1,0:T(8,128)(2,1)} %param.11) | copy-start | bytes 1179652
  13.9 1.0 %copy-start.4 = (bf16[4,256,192]{2,1,0:T(8,128)(2,1)S(1)}, bf16[4,256,192]{2,1,0:T(8,128)(2,1)}, u32[]{:S(2)}) copy-start(bf16[4,256,192]{2,1,0:T(8,128)(2,1)} %copy-done.3) | copy-start | bytes 1179652
  39.7 0.8 copy-start.5
  40.4 0.8 copy-start.7
  41.3 25.4 %copy-start.8 = (bf16[4,256,192]{2,1,0:T(8,128)(2,1)S(1)}, bf16[4,256,192]{2,1,0:T(8,128)(2,1)}, u32[]{:S(2)}) copy-start(bf16[4,256,192]{2,1,0:T(8,128)(2,1)} %copy-done.7) | copy-start | bytes 1179652
  41.3 27.8 %copy-start.6 = (bf16[4,256,192]{2,1,0:T(8,128)(2,1)S(1)}, bf16[4,256,192]{2,1,0:T(8,128)(2,1)}, u32[]{:S(2)}) copy-start(bf16[4,256,192]{2,1,0:T(8,128)(2,1)} %copy-done.5) | copy-start | bytes 1179652
  41.3 6.3 %collective-permute-start.4 = (bf16[1280,128]{1,0:T(8,128)(2,1)S(1)}, bf16[1280,128]{1,0:T(8,128)(2,1)S(1)}, u32[]{:S(2)}, u32[]{:S(2)}) collective-permute-start(bf16[1280,128]{1,0:T(8,128)(2,1)S(1)} %dynamic-slice_bitcast_fusion), channel_id=1, source_target_pairs={{0,1},{1,0},{2,3},{3,2},{4,5},{5,4},{6,7},{7,6},{8,9},{9,8},{10,11... | collective-permute-start | bytes 983048 | tf_op jit(solution)/shard_map/ppermute | solution.py:387
  47.7 43.7 %copy-start.9 = (f32[4,256,192]{2,1,0:T(8,128)S(1)}, f32[4,256,192]{2,1,0:T(8,128)}, u32[]{:S(2)}) copy-start(f32[4,256,192]{2,1,0:T(8,128)} %get-tuple-element.14) | copy-start | bytes 2359300
  61.0 14.1 %all-to-all-start.1 = ((bf16[8,80,128]{2,1,0:T(8,128)(2,1)}), bf16[8,80,128]{2,1,0:T(8,128)(2,1)S(1)}, u32[]{:S(2)}, u32[]{:S(2)}) async-start(bf16[8,80,128]{2,1,0:T(8,128)(2,1)} %broadcast_in_dim.7), calls=%async_computation.1 | async-start | bytes 327680 | tf_op jit(solution)/shard_map/all_to_all | solution.py:376
  66.7 24.7 %collective-permute-start.2 = (bf16[4,256,192]{2,1,0:T(8,128)(2,1)S(1)}, bf16[4,256,192]{2,1,0:T(8,128)(2,1)S(1)}, u32[]{:S(2)}, u32[]{:S(2)}) collective-permute-start(bf16[4,256,192]{2,1,0:T(8,128)(2,1)S(1)} %copy-done.8), channel_id=1, source_target_pairs={{1,0},{2,1},{3,2},{4,3},{5,4},{6,5},{7,6},{8,7},{9,8},{10,9},{11,1... | collective-permute-start | bytes 1179656 | tf_op jit(solution)/shard_map/ppermute | solution.py:457
  69.0 22.4 %collective-permute-start.3 = (bf16[4,256,192]{2,1,0:T(8,128)(2,1)S(1)}, bf16[4,256,192]{2,1,0:T(8,128)(2,1)}, u32[]{:S(2)}, u32[]{:S(2)}) collective-permute-start(bf16[4,256,192]{2,1,0:T(8,128)(2,1)S(1)} %copy-done.6), channel_id=1, source_target_pairs={{0,1},{1,2},{2,3},{3,4},{4,5},{5,6},{6,7},{7,8},{8,9},{9,10},{10,1... | collective-permute-start | bytes 1179656 | tf_op jit(solution)/shard_map/ppermute | solution.py:458
  86.4 7.0 %collective-permute-start.5 = (bf16[1280,128]{1,0:T(8,128)(2,1)S(1)}, bf16[1280,128]{1,0:T(8,128)(2,1)S(1)}, u32[]{:S(2)}, u32[]{:S(2)}) collective-permute-start(bf16[1280,128]{1,0:T(8,128)(2,1)S(1)} %bitcast.63), channel_id=1, source_target_pairs={{0,1},{1,0},{2,3},{3,2},{4,5},{5,4},{6,7},{7,6},{8,9},{9,8},{10,11... | collective-permute-start | bytes 983048 | tf_op jit(solution)/shard_map/ppermute | solution.py:394
  94.9 0.9 copy-start.12
  95.0 0.9 copy-start.11

commit v2 on v1

v2 whole, which is shorter than its diff:
```python
import math

import jax
import jax.numpy as jnp
from jax import lax
from jax.experimental import pallas as pl
from jax.experimental.pallas import tpu as pltpu
from jax.sharding import Mesh, PartitionSpec as P

GELU_C = math.sqrt(2.0 / math.pi)
EPSILON = 1e-06
F32 = jnp.float32
BF16 = jnp.bfloat16
T = 4
S = 16
PX = S * S
C = 192
HID = 768
W = 24
DW = 32
WEIGHT_ROWS = 2 * C * HID // 128
ROWS = 2560
HALF = ROWS // 2
MIB = 1024 * 1024
VMEM_LIMIT = 60 * MIB
SLABS = 3 * T // 2
BLOCKS = 32


def gelu_pair(value):
    square = value * value
    half = 0.5 + 0.5 * jnp.tanh(value * (GELU_C + GELU_C * 0.044715 * square))
    result = value * half
    slope = half + result * (1.0 - half) * (2.0 * GELU_C + GELU_C * 6.0 * 0.044715 * square)
    return (result, slope)


def turn_of(quarter):
    on_i = jnp.where(quarter == 0, S, jnp.where(quarter == 1, -1, jnp.where(quarter == 2, -S, 1)))
    on_j = jnp.where(quarter == 0, 1, jnp.where(quarter == 1, S, jnp.where(quarter == 2, -1, -S)))
    base = jnp.where(
        quarter == 0, 0, jnp.where(quarter == 1, S - 1, jnp.where(quarter == 2, PX - 1, PX - S))
    )
    return on_i, on_j, base


SLOTS = (
    (0, S - 3, -3, 3, 19),
    (2, 0, -3, 3, 19),
    (1, 0, S - 3, 0, 3),
    (1, 0, -19, 19, 22),
    (0, S - 3, S - 3, 0, 3),
    (0, S - 3, -19, 19, 22),
    (2, 0, S - 3, 0, 3),
    (2, 0, -19, 19, 22),
)
FIRST = (0, 3, 19)
COUNT = (3, S, 3)


def slot_match(slot, quarter, transposed):
    group, row0, col0, low, high = SLOTS[slot]
    length = COUNT[group] * W
    shape = (PX, length) if transposed else (length, PX)
    along = 1 if transposed else 0
    line = (1, length) if transposed else (length, 1)
    place = lax.broadcasted_iota(jnp.int32, line, along)
    row = place // W
    col = place - row * W
    on_i, on_j, base = turn_of(quarter)
    source = on_i * (row + row0) + on_j * (col + col0) + base
    source = jnp.where((col >= low) & (col < high), source, -1)
    return (lax.broadcasted_iota(jnp.int32, shape, 1 - along) == source).astype(F32).astype(BF16)


def block_places(block):
    place = lax.broadcasted_iota(jnp.int32, (8 * S, 1), 0)
    row = place // 8
    return row, place - row * 8 + 8 * block


def matches(source):
    at = lax.broadcasted_iota(jnp.int32, (8 * S, PX), 1)
    return (at == source).astype(F32).astype(BF16)


def centre_match(block):
    row, col = block_places(block)
    return matches(jnp.where((col >= 3) & (col < S + 3), row * S + col - 3, -1))


def side_match(slot, quarter):
    _, row0, col0, low, high = SLOTS[slot]
    row, col = block_places(0 if slot == 2 else 2)
    on_i, on_j, base = turn_of(quarter)
    source = on_i * (row + row0) + on_j * (col + col0) + base
    return matches(jnp.where((col >= low) & (col < high), source, -1))


def lane_is_low():
    return lax.broadcasted_iota(jnp.int32, (1, 128), 1) < 64


def packed_slabs(x):
    first = x[:, :128]
    rest = jnp.concatenate([x[:, 128:], jnp.zeros((x.shape[0], 64), x.dtype)], axis=1)
    crossed = pltpu.roll(first, 64, 1)
    low = lane_is_low()
    return first, jnp.where(low, rest, crossed), jnp.where(low, crossed, pltpu.roll(rest, 64, 1))


def prepare_kernel(
    near_hbm,
    rot_hbm,
    owner_hbm,
    own_hbm,
    up_hbm,
    kernel_hbm,
    gain_hbm,
    bias_hbm,
    up_bias_hbm,
    where_ref,
    own_ref,
    kern,
    up_ref,
    gain_ref,
    bias_ref,
    up_bias_ref,
    near_ref,
    rot_ref,
    owner_ref,
    own_raw,
    up_raw,
    kernel_ref,
    gain_in,
    bias_in,
    up_bias_in,
    ids,
    sems,
):
    copies = [
        pltpu.make_async_copy(a, b, sems.at[k])
        for k, (a, b) in enumerate(
            (
                (near_hbm, near_ref),
                (rot_hbm, rot_ref),
                (owner_hbm, owner_ref),
                (own_hbm, own_raw),
                (up_hbm, up_raw),
                (kernel_hbm, kernel_ref),
                (gain_hbm, gain_in),
                (bias_hbm, bias_in),
                (up_bias_hbm, up_bias_in),
            )
        )
    ]
    for copy in copies:
        copy.start()
    for copy in copies:
        copy.wait()

    position = (lax.axis_index("xh") * 8 + lax.axis_index("z")) * 2 + lax.axis_index("c")
    first = position * T

    @pl.loop(0, 128, unroll=8)
    def _(q):
        at = owner_ref[q] - first

        @pl.when((at >= 0) & (at < T))
        def _():
            ids[at] = q

    for tile in range(T):
        for slot in range(8):
            row = owner_ref[near_ref[slot, ids[tile]]]
            block = lax.rem(row // T - position + 1 + BLOCKS, BLOCKS)
            where_ref[tile * 8 + slot] = block * T + lax.rem(row, T)
            where_ref[T * 8 + tile * 8 + slot] = rot_ref[slot, ids[tile]]

    own_ref[:, :, :C] = own_raw[...]
    own_ref[:, :, C:] = jnp.zeros((T, PX, 256 - C), BF16)
    for part, value in enumerate(packed_slabs(gain_in[...].reshape(1, C))):
        gain_ref[part] = value
    for part, value in enumerate(packed_slabs(bias_in[...].reshape(1, C))):
        bias_ref[part] = value
    up_bias_ref[...] = up_bias_in[...].reshape(1, HID)
    for a in range(7):
        for part, value in enumerate(packed_slabs(kernel_ref[a])):
            for b in range(7):
                tap = jnp.broadcast_to(value[b : b + 1], (8, 128))
                kern[part, 8 * (a * 7 + b) : 8 * (a * 7 + b + 1), :] = tap
    up_ref[0, :C, :] = up_raw[...]
    up_ref[0, C:, :] = jnp.zeros((64, HID), BF16)
    up_ref[1, :64, :] = jnp.zeros((64, HID), BF16)
    up_ref[1, 64:, :] = up_raw[...]


def run_prepare(*args):
    vmem = pl.BlockSpec(memory_space=pltpu.VMEM)
    smem = pl.BlockSpec(memory_space=pltpu.SMEM)
    hbm = pl.BlockSpec(memory_space=pltpu.HBM)
    return pl.pallas_call(
        prepare_kernel,
        out_shape=(
            jax.ShapeDtypeStruct((T * 16,), jnp.int32),
            jax.ShapeDtypeStruct((T, PX, 256), BF16),
            jax.ShapeDtypeStruct((3, 8 * 49, 128), F32),
            jax.ShapeDtypeStruct((2, 256, HID), BF16),
            jax.ShapeDtypeStruct((3, 1, 128), F32),
            jax.ShapeDtypeStruct((3, 1, 128), F32),
            jax.ShapeDtypeStruct((1, HID), F32),
        ),
        in_specs=[hbm] * 9,
        out_specs=(smem,) + (vmem,) * 6,
        scratch_shapes=[
            pltpu.SMEM((8, 128), jnp.int32),
            pltpu.SMEM((8, 128), jnp.int32),
            pltpu.SMEM((128,), jnp.int32),
            pltpu.VMEM((T, PX, C), BF16),
            pltpu.VMEM((C, HID), BF16),
            pltpu.VMEM((7, 7, C), F32),
            pltpu.VMEM((C,), F32),
            pltpu.VMEM((C,), F32),
            pltpu.VMEM((HID,), F32),
            pltpu.SMEM((T,), jnp.int32),
            pltpu.SemaphoreType.DMA((9,)),
        ],
        compiler_params=pltpu.CompilerParams(vmem_limit_bytes=VMEM_LIMIT),
        cost_estimate=pl.CostEstimate(flops=10**8, bytes_accessed=6 * 10**6, transcendentals=0),
    )(*args)


def forward_kernel(
    where_hbm,
    prev_hbm,
    next_hbm,
    own_hbm,
    cot_hbm,
    down_hbm,
    up_hbm,
    kern_hbm,
    gain_hbm,
    bias_hbm,
    up_bias_hbm,
    updated_hbm,
    dmix_hbm,
    send_ref,
    keep_ref,
    where_ref,
    raw,
    cot_ref,
    down_ref,
    up_ref,
    kern,
    gain_ref,
    bias_ref,
    up_bias_ref,
    out_ref,
    dmix,
    src,
    pad,
    mix,
    xhat,
    inv,
    normed,
    g_up_bias,
    g_small,
    grads_ref,
    up_ref32,
    back_ref32,
    act_ref,
    d_up_ref,
    sems,
):
    low_half = lane_is_low()
    core = lax.axis_index("c")
    copies = [
        pltpu.make_async_copy(a, b, sems.at[k])
        for k, (a, b) in enumerate(
            (
                (where_hbm, where_ref),
                (prev_hbm, raw.at[0:T]),
                (next_hbm, raw.at[T:]),
                (own_hbm, src.at[T : 2 * T]),
                (kern_hbm, kern),
                (gain_hbm, gain_ref),
                (bias_hbm, bias_ref),
                (up_hbm, up_ref),
                (down_hbm, down_ref),
                (cot_hbm, cot_ref),
                (up_bias_hbm, up_bias_ref),
            )
        )
    ]
    for copy in copies:
        copy.start()
    src[0:T, :, C:] = jnp.zeros((T, PX, 256 - C), BF16)
    src[2 * T :, :, C:] = jnp.zeros((T, PX, 256 - C), BF16)
    g_up_bias[...] = jnp.zeros_like(g_up_bias)
    g_small[...] = jnp.zeros_like(g_small)
    dmix[...] = jnp.zeros_like(dmix)
    grads_ref[...] = jnp.zeros_like(grads_ref)
    for copy in copies[:4]:
        copy.wait()
    src[0:T, :, :C] = raw[0:T]
    src[2 * T :, :, :C] = raw[T:]

    def put_rows(pair, half, start, count, value):
        rows = pl.ds(start, count)
        if half == 0:
            pad[pair * 3, rows, :] = value[:, :128]
            pad[pair * 3 + 1, rows, :] = value[:, 128:]
        else:
            pad[pair * 3 + 1, rows, :] += value[:, :128]
            pad[pair * 3 + 2, rows, :] = value[:, 128:]

    def put(pair, half, start, count, value):
        put_rows(pair, half, start, count, value if half == 0 else pltpu.roll(value, 64, 1))

    @pl.loop(0, T // 2)
    def _(pair):
        for half in range(2):
            tile = pair * 2 + half
            for group in (0, 2):
                total = None
                for slot in range(8):
                    if SLOTS[slot][0] != group:
                        continue
                    match = slot_match(slot, where_ref[T * 8 + tile * 8 + slot], False)
                    piece = jnp.dot(
                        match, src[where_ref[tile * 8 + slot]], preferred_element_type=F32
                    )
                    total = piece if total is None else total + piece
                put(pair, half, FIRST[group] * W, COUNT[group] * W, total)
            for block in range(3):
                total = jnp.dot(centre_match(block), src[T + tile], preferred_element_type=F32)
                if block != 1:
                    slot = 2 + block // 2
                    match = side_match(slot, where_ref[T * 8 + tile * 8 + slot])
                    total += jnp.dot(
                        match, src[where_ref[tile * 8 + slot]], preferred_element_type=F32
                    )
                if half == 1:
                    total = pltpu.roll(total, 64, 1)
                for i in range(S):
                    put_rows(pair, half, (i + 3) * W + 8 * block, 8, total[8 * i : 8 * i + 8])

    for copy in copies[4:7]:
        copy.wait()

    @pl.loop(0, 3 * T // 2)
    def _(slab):
        part = lax.rem(slab, 3)
        for half in range(2):
            for b in range(7):
                acc = [None] * S
                taps = [kern[part, pl.ds(8 * (a * 7 + b), 8), :] for a in range(7)]
                for m in range(S + 6):
                    x = pad[slab, pl.ds(m * W + b + 8 * half, 8), :]
                    for a in range(7):
                        i = m - a
                        if 0 <= i < S:
                            term = x * taps[a]
                            acc[i] = term if acc[i] is None else acc[i] + term
                for i in range(S):
                    rows = pl.ds(i * S + 8 * half, 8)
                    mix[slab, rows, :] = acc[i] if b == 0 else mix[slab, rows, :] + acc[i]

    def pair_means(s0, s1, s2):
        first = jnp.sum(s0 + jnp.where(low_half, s1, 0.0), axis=1, keepdims=True) * (1.0 / C)
        second = jnp.sum(s2 + jnp.where(low_half, 0.0, s1), axis=1, keepdims=True) * (1.0 / C)
        return first, jnp.where(low_half, first, second), second

    CH = 64

    @pl.loop(0, (T // 2) * (PX // CH), unroll=4)
    def _(step):
        pair = step // (PX // CH)
        rows = pl.ds(pl.multiple_of(lax.rem(step, PX // CH) * CH, CH), CH)
        slabs = [mix[pair * 3 + k, rows, :] for k in range(3)]
        means = pair_means(*slabs)
        slabs = [x - m for x, m in zip(slabs, means)]
        spreads = pair_means(*[x * x for x in slabs])
        for k in range(3):
            deviation = jnp.broadcast_to(lax.rsqrt(spreads[k] + EPSILON), (CH, 128))
            standard = slabs[k] * deviation
            inv[pair * 3 + k, rows, :] = deviation
            xhat[pair * 3 + k, rows, :] = standard
            normed[pair, rows, 128 * k : 128 * (k + 1)] = (
                standard * gain_ref[k] + bias_ref[k]
            ).astype(BF16)

    for copy in copies[7:]:
        copy.wait()

    @pl.loop(0, T // 2)
    def _(pair):
        normed_grads = []
        for half in range(2):
            tile = pair * 2 + half
            x = normed[pair, :, 128 * half : 128 * half + 256]
            x_t = jnp.transpose(x.astype(F32)).astype(BF16)
            cot = cot_ref[tile]
            cot_t = jnp.transpose(cot.astype(F32)).astype(BF16)
            branch = jnp.zeros((PX, C), F32)
            normed_grad = jnp.zeros((PX, 256), F32)
            for chunk in range(3):
                hid = slice(256 * chunk, 256 * (chunk + 1))
                up_ref32[...] = jnp.dot(x, up_ref[half, :, hid], preferred_element_type=F32)
                back_ref32[...] = jnp.dot(cot, down_ref[:, hid], preferred_element_type=F32)
                bias_sum = jnp.zeros((8, 256), F32)
                for r in range(0, PX, 16):
                    rows = slice(r, r + 16)
                    value, slope = gelu_pair(up_ref32[rows, :] + up_bias_ref[:, hid])
                    d_up = back_ref32[rows, :] * slope
                    bias_sum += d_up[:8] + d_up[8:]
                    act_ref[rows, :] = value.astype(BF16)
                    d_up_ref[rows, :] = d_up.astype(BF16)
                g_up_bias[:, hid] += bias_sum
                activation = act_ref[...]
                d_up_b = d_up_ref[...]
                branch += times_transposed(activation, down_ref[:, hid])
                down_grad = jnp.dot(cot_t, activation, preferred_element_type=F32)
                up_grad = jnp.dot(x_t, d_up_b, preferred_element_type=F32)
                for k in range(2):
                    at = C * (2 * chunk + k)
                    lanes = slice(128 * k, 128 * (k + 1))
                    grads_ref[at : at + C, :] += up_grad[64 * half : 64 * half + C, lanes]
                    at += WEIGHT_ROWS // 2
                    grads_ref[at : at + C, :] += down_grad[:, lanes]
                normed_grad += times_transposed(d_up_b, up_ref[half, :, hid])
            out_ref[tile] = (src[T + tile, :, :C].astype(F32) + branch).astype(BF16)
            normed_grads.append(normed_grad)
        mix[pair * 3] = normed_grads[0][:, :128]
        mix[pair * 3 + 1] = normed_grads[0][:, 128:] + normed_grads[1][:, :128]
        mix[pair * 3 + 2] = normed_grads[1][:, 128:]

    @pl.loop(0, (T // 2) * (PX // CH), unroll=4)
    def _(step):
        pair = step // (PX // CH)
        start = pl.multiple_of(lax.rem(step, PX // CH) * CH, CH)
        rows = pl.ds(start, CH)
        grads = [mix[pair * 3 + k, rows, :] for k in range(3)]
        standard = [xhat[pair * 3 + k, rows, :] for k in range(3)]
        for k in range(3):
            g_small[k, 8 * 49 : 8 * 50, :] += jnp.sum(
                (grads[k] * standard[k]).reshape(CH // 8, 8, 128), axis=0
            )
            g_small[k, 8 * 50 : 8 * 51, :] += jnp.sum(grads[k].reshape(CH // 8, 8, 128), axis=0)
        scaled = [grads[k] * gain_ref[k] for k in range(3)]
        means = pair_means(*scaled)
        products = pair_means(*[e * x for e, x in zip(scaled, standard)])
        for k in range(3):
            d_mixed = inv[pair * 3 + k, rows, :] * (
                scaled[k] - means[k] - standard[k] * products[k]
            )
            for r in range(CH // S):
                at = (start // S + r) * DW + 8
                dmix[pair * 3 + k, pl.ds(pl.multiple_of(at, 8), S), :] = d_mixed[r * S : (r + 1) * S]

    results = [
        pltpu.make_async_copy(out_ref, updated_hbm, sems.at[11]),
        pltpu.make_async_copy(dmix, dmix_hbm, sems.at[12]),
    ]
    for result in results:
        result.start()

    @pl.loop(0, 3 * T // 2)
    def _(slab):
        part = lax.rem(slab, 3)
        for half in range(2):
            grads = [dmix[slab, pl.ds(i * DW + 8 + 8 * half, 8), :] for i in range(S)]
            for b in range(7):
                acc = [None] * 7
                for m in range(S + 6):
                    x = pad[slab, pl.ds(m * W + b + 8 * half, 8), :]
                    for a in range(7):
                        i = m - a
                        if 0 <= i < S:
                            term = x * grads[i]
                            acc[a] = term if acc[a] is None else acc[a] + term
                for a in range(7):
                    g_small[part, 8 * (a * 7 + b) : 8 * (a * 7 + b + 1), :] += acc[a]
    sums = [jnp.sum(g_small[k].reshape(56, 8, 128), axis=1) for k in range(3)]
    crossed = pltpu.roll(jnp.where(low_half, sums[2], sums[1]), 64, 1)
    grads_ref[WEIGHT_ROWS : WEIGHT_ROWS + 56, :] = (sums[0] + crossed)
    grads_ref[WEIGHT_ROWS + 56 : WEIGHT_ROWS + 112, :] = (
        sums[1] + pltpu.roll(sums[2], 64, 1)
    )
    bias_sum = jnp.sum(g_up_bias[...], axis=0, keepdims=True)
    bias_rows = jnp.concatenate(
        [bias_sum[:, 128 * k : 128 * (k + 1)] for k in range(6)] + [jnp.zeros((10, 128), F32)],
        axis=0,
    )
    grads_ref[WEIGHT_ROWS + 112 : WEIGHT_ROWS + 128, :] = bias_rows
    send_ref[...] = grads_ref[pl.ds((1 - core) * HALF, HALF), :].astype(BF16)
    keep_ref[...] = grads_ref[pl.ds(core * HALF, HALF), :]
    for result in results:
        result.wait()


def times_transposed(x, y):
    return lax.dot_general(x, y, (((1,), (1,)), ((), ())), preferred_element_type=F32)


def run_forward(*args):
    vmem = pl.BlockSpec(memory_space=pltpu.VMEM)
    hbm = pl.BlockSpec(memory_space=pl.ANY)
    slab = pltpu.VMEM((SLABS, PX, 128), F32)
    return pl.pallas_call(
        forward_kernel,
        out_shape=(
            jax.ShapeDtypeStruct((T, PX, C), BF16),
            jax.ShapeDtypeStruct((SLABS, S * DW, 128), F32),
            jax.ShapeDtypeStruct((HALF, 128), BF16),
            jax.ShapeDtypeStruct((HALF, 128), F32),
        ),
        in_specs=[hbm] * 11,
        out_specs=(hbm, hbm, vmem, vmem),
        scratch_shapes=[
            pltpu.SMEM((T * 16,), jnp.int32),
            pltpu.VMEM((2 * T, PX, C), BF16),
            pltpu.VMEM((T, PX, C), BF16),
            pltpu.VMEM((C, HID), BF16),
            pltpu.VMEM((2, 256, HID), BF16),
            pltpu.VMEM((3, 8 * 49, 128), F32),
            pltpu.VMEM((3, 1, 128), F32),
            pltpu.VMEM((3, 1, 128), F32),
            pltpu.VMEM((1, HID), F32),
            pltpu.VMEM((T, PX, C), BF16),
            pltpu.VMEM((SLABS, S * DW, 128), F32),
            pltpu.VMEM((3 * T, PX, 256), BF16),
            pltpu.VMEM((SLABS, 22 * W, 128), F32),
            slab,
            slab,
            slab,
            pltpu.VMEM((T // 2, PX, 384), BF16),
            pltpu.VMEM((8, HID), F32),
            pltpu.VMEM((3, 8 * 56, 128), F32),
            pltpu.VMEM((ROWS, 128), F32),
            pltpu.VMEM((PX, 256), F32),
            pltpu.VMEM((PX, 256), F32),
            pltpu.VMEM((PX, 256), BF16),
            pltpu.VMEM((PX, 256), BF16),
            pltpu.SemaphoreType.DMA((13,)),
        ],
        compiler_params=pltpu.CompilerParams(vmem_limit_bytes=55 * MIB),
        cost_estimate=pl.CostEstimate(flops=4 * 10**9, bytes_accessed=8 * 10**6, transcendentals=10**6),
    )(*args)


def spread_kernel(dmix, kern, dpad):
    @pl.loop(0, SLABS)
    def _(slab):
        part = lax.rem(slab, 3)
        for third in range(3):
            for b in range(7):
                acc = [None] * (S + 6)
                taps = [kern[part, pl.ds(8 * (a * 7 + b), 8), :] for a in range(7)]
                for i in range(S):
                    x = dmix[slab, pl.ds(i * DW + 8 + 8 * third - b, 8), :]
                    for a in range(7):
                        term = x * taps[a]
                        acc[i + a] = term if acc[i + a] is None else acc[i + a] + term
                for m in range(S + 6):
                    rows = pl.ds(m * W + 8 * third, 8)
                    dpad[slab, rows, :] = acc[m] if b == 0 else dpad[slab, rows, :] + acc[m]


def run_spread(dmix, taps):
    vmem = pl.BlockSpec(memory_space=pltpu.VMEM)
    return pl.pallas_call(
        spread_kernel,
        out_shape=jax.ShapeDtypeStruct((SLABS, 22 * W, 128), F32),
        in_specs=[vmem] * 2,
        out_specs=vmem,
        compiler_params=pltpu.CompilerParams(vmem_limit_bytes=VMEM_LIMIT),
        cost_estimate=pl.CostEstimate(flops=10**9, bytes_accessed=5 * 10**6, transcendentals=0),
    )(dmix, taps)


def return_kernel(
    where_ref, dpad, cot_hbm, part_ref, to_prev_ref, to_next_ref, collected, cot_ref, sem
):
    copy = pltpu.make_async_copy(cot_hbm, cot_ref, sem)
    copy.start()
    collected[...] = jnp.zeros_like(collected)

    @pl.loop(0, T // 2)
    def _(pair):
        for half in range(2):
            tile = pair * 2 + half
            for slot in range(8):
                group = SLOTS[slot][0]
                rows = pl.ds(FIRST[group] * W, COUNT[group] * W)
                border = jnp.concatenate(
                    [dpad[pair * 3 + half + k, rows, :] for k in range(2)], axis=1
                ).astype(BF16)
                match = slot_match(slot, where_ref[T * 8 + tile * 8 + slot], True)
                piece = jnp.dot(match, border, preferred_element_type=F32)
                if half == 1:
                    piece = pltpu.roll(piece, 192, 1)
                collected[where_ref[tile * 8 + slot]] += piece

    to_prev_ref[...] = collected[0:T, :, :C].astype(BF16)
    to_next_ref[...] = collected[2 * T :, :, :C].astype(BF16)
    copy.wait()

    @pl.loop(0, T // 2)
    def _(pair):
        for half in range(2):
            tile = pair * 2 + half
            for i in range(S):
                rows = slice(i * S, (i + 1) * S)
                centre = jnp.concatenate(
                    [dpad[pair * 3 + half + k, pl.ds((i + 3) * W + 3, S), :] for k in range(2)],
                    axis=1,
                )
                if half == 1:
                    centre = pltpu.roll(centre, 192, 1)
                part_ref[tile, rows, :] = (
                    cot_ref[tile, rows, :].astype(F32)
                    + centre[:, :C]
                    + collected[T + tile, rows, :C]
                )


def run_return(where, dpad, cot):
    vmem = pl.BlockSpec(memory_space=pltpu.VMEM)
    smem = pl.BlockSpec(memory_space=pltpu.SMEM)
    tile = (T, PX, C)
    return pl.pallas_call(
        return_kernel,
        out_shape=(
            jax.ShapeDtypeStruct(tile, F32),
            jax.ShapeDtypeStruct(tile, BF16),
            jax.ShapeDtypeStruct(tile, BF16),
        ),
        in_specs=[smem, vmem, pl.BlockSpec(memory_space=pltpu.HBM)],
        out_specs=(vmem,) * 3,
        scratch_shapes=[
            pltpu.VMEM((3 * T, PX, 256), F32),
            pltpu.VMEM((T, PX, C), BF16),
            pltpu.SemaphoreType.DMA,
        ],
        compiler_params=pltpu.CompilerParams(vmem_limit_bytes=VMEM_LIMIT),
        cost_estimate=pl.CostEstimate(flops=10**9, bytes_accessed=5 * 10**6, transcendentals=0),
    )(where, dpad, cot)


def finish_kernel(
    core_ref, mine_ref, other_ref, up_out, down_out, kernel_out, gain_out, bias_out, up_bias_out, halves
):
    scale = 1.0 / math.sqrt(8 * BLOCKS * T * PX)
    core = core_ref[0]
    halves[core] = mine_ref[...]
    halves[1 - core] = other_ref[...]

    def rows(start, count):
        side, at = divmod(start, HALF)
        if at + count <= HALF:
            return halves[side, at : at + count, :].astype(F32) * scale
        split = HALF - at
        return jnp.concatenate([rows(start, split), rows(start + split, count - split)], axis=0)

    for k in range(HID // 128):
        up_out[:, 128 * k : 128 * (k + 1)] = rows(C * k, C)
        down_out[:, 128 * k : 128 * (k + 1)] = rows(WEIGHT_ROWS // 2 + C * k, C)
    small = jnp.concatenate(
        [rows(WEIGHT_ROWS, 56), rows(WEIGHT_ROWS + 56, 56)[:, :64]], axis=1
    )
    for a in range(7):
        kernel_out[a] = small[7 * a : 7 * (a + 1)]
    gain_out[...] = small[49:50].reshape(C)
    bias_out[...] = small[50:51].reshape(C)
    bias = rows(WEIGHT_ROWS + 112, 16)
    for k in range(HID // 128):
        up_bias_out[128 * k : 128 * (k + 1)] = bias[k : k + 1].reshape(128)


def run_finish(core, mine, other):
    vmem = pl.BlockSpec(memory_space=pltpu.VMEM)
    smem = pl.BlockSpec(memory_space=pltpu.SMEM)
    return pl.pallas_call(
        finish_kernel,
        out_shape=(
            jax.ShapeDtypeStruct((C, HID), F32),
            jax.ShapeDtypeStruct((C, HID), F32),
            jax.ShapeDtypeStruct((7, 7, C), F32),
            jax.ShapeDtypeStruct((C,), F32),
            jax.ShapeDtypeStruct((C,), F32),
            jax.ShapeDtypeStruct((HID,), F32),
        ),
        in_specs=[smem, vmem, vmem],
        out_specs=(vmem,) * 6,
        scratch_shapes=[pltpu.VMEM((2, HALF, 128), BF16)],
        compiler_params=pltpu.CompilerParams(vmem_limit_bytes=8 * MIB),
        cost_estimate=pl.CostEstimate(flops=10**6, bytes_accessed=2 * 10**6, transcendentals=0),
    )(core, mine, other)


def shared_with(x, axes, count):
    return lax.all_to_all(jnp.broadcast_to(x[None], (count,) + x.shape), axes, 0, 0)


def total_of(x):
    return jnp.sum(x.astype(F32), axis=0)


def on_device(
    fields,
    depth_kernel,
    layer_norm_gain,
    layer_norm_bias,
    up_weight,
    up_bias,
    down_weight,
    cotangent,
    neighbours,
    rotation,
    tile_owner,
):
    around = ("xh", "z", "c")
    plane = ("y", "xl", "xh")
    swap = [(0, 1), (1, 0)]
    to_right = [(i, (i + 1) % BLOCKS) for i in range(BLOCKS)]
    to_left = [((i + 1) % BLOCKS, i) for i in range(BLOCKS)]
    own = fields.reshape(T, PX, C)
    cot = cotangent.reshape(T, PX, C)
    prev = lax.ppermute(own, around, to_right)
    nxt = lax.ppermute(own, around, to_left)
    where, wide, taps, up, gain, bias, up_bias = run_prepare(
        neighbours.T,
        rotation.T,
        tile_owner,
        own,
        up_weight,
        depth_kernel,
        layer_norm_gain,
        layer_norm_bias,
        up_bias,
    )
    updated, dmix, send, keep = run_forward(
        where, prev, nxt, wide, cot, down_weight.T, up, taps, gain, bias, up_bias
    )
    mine = (keep + lax.ppermute(send, "c", swap).astype(F32)).astype(BF16)
    dmix, mine = lax.optimization_barrier((dmix, mine))
    mine = lax.all_to_all(mine.reshape(16, HALF // 16, 128), plane, 0, 0)
    dpad = run_spread(dmix, taps)
    dpad, mine = lax.optimization_barrier((dpad, mine))
    mine = total_of(mine).astype(BF16)
    dpad, mine = lax.optimization_barrier((dpad, mine))
    mine = shared_with(mine, "z", 8)
    part, to_prev, to_next = run_return(where, dpad, cot)
    mine, to_prev, to_next = lax.optimization_barrier((mine, to_prev, to_next))
    from_right = lax.ppermute(to_prev, around, to_left)
    from_left = lax.ppermute(to_next, around, to_right)
    mine = total_of(mine).astype(BF16)
    mine = shared_with(mine, plane, 16)
    grad_fields = (part + from_right.astype(F32) + from_left.astype(F32)).astype(BF16)
    mine, grad_fields = lax.optimization_barrier((mine, grad_fields))
    mine = mine.reshape(HALF, 128)
    other = lax.ppermute(mine, "c", swap)
    core = lax.axis_index("c").astype(jnp.int32).reshape(1)
    grad_up, grad_down_t, grad_kernel, grad_gain, grad_bias, grad_up_bias = run_finish(
        core, mine, other
    )
    return (
        updated.reshape(fields.shape),
        grad_fields.reshape(fields.shape),
        grad_kernel,
        grad_gain,
        grad_bias,
        grad_up,
        grad_up_bias,
        grad_down_t.T,
    )


def solution(mesh):
    fine = Mesh(mesh.devices.reshape(4, 2, 2, 8, 2), ("y", "xl", "xh", "z", "c"))
    tiles = P(("y", "xl"), ("xh", "z", "c"), None, None, None)
    return jax.shard_map(
        on_device,
        mesh=fine,
        in_specs=(tiles, P(), P(), P(), P(), P(), P(), tiles, P(), P(), P()),
        out_specs=(tiles, tiles, P(), P(), P(), P(), P(), P()),
        check_vma=False,
    )
```

time: 96.5 us -> 86.8 us (0.90)
  blocking collectives: 23.8 us -> 0 us
  waiting for transfers between devices: 6.71 us -> 22.1 us
  local copies, waits for them, and re-layouts: 9.87 us -> 2.25 us
  Pallas kernels: 24.7 us -> 31.2 us
  starting transfers between devices: 23.2 us -> 27.2 us
  other arithmetic: 6.71 us -> 2.92 us
    all_to_all x2 -> x0, blocking collectives: 23.8 us -> none  [the longest x1 12.5 us: sum_everywhere(): lax.all_to_all(mine.reshape(16, ROWS // 32, 128), plane, 0, 0)]
    pallas_call x1 -> x5, Pallas kernels: 24.7 us -> 31.2 us  [the longest x1 15.3 us: run_forward(): pl.pallas_call(forward_kernel, out_shape=(jax.ShapeDtypeStruct((T, PX, C)...]
    unnamed x44 -> x6, local copies, waits for them, and re-layouts: 6.78 us -> 0.8 us
    all_to_all x1 -> x2, waiting for transfers between devices: 4.38 us -> 9.64 us  [shared_with(): lax.all_to_all(jnp.broadcast_to(x[None], (count,) + x.shape), axes, 0, 0)]
    ppermute x2, starting transfers between devices: 10.1 us -> 5 us  [the longest x1 4.46 us: on_device(): mine = (keep + lax.ppermute(send, 'c', swap).astype(F32)).astype(BF16)]
    all_to_all x0 -> x1, starting transfers between devices: none -> 4.87 us  [on_device(): mine = lax.all_to_all(mine.reshape(16, HALF // 16, 128), plane, 0, 0)]
    all_to_all x1 -> x2, starting transfers between devices: 5.67 us -> 10.4 us  [shared_with(): lax.all_to_all(jnp.broadcast_to(x[None], (count,) + x.shape), axes, 0, 0)]
    ppermute x1, waiting for transfers between devices: 0.01 us -> 3.49 us  [on_device(): prev = lax.ppermute(own, around, to_right)]
  transfers between devices with their start and end apart: 7 -> 9, of which waited for: 3 -> 8; matrix products, arithmetic and copies ran while one was open for 8% -> 2% of each run, Pallas kernels for 0% -> 17%
where the time goes in v2:
time: 86.8 us; the launch traced here: 86.3 us
  Pallas kernels  31.2 us (36%)
  starting transfers between devices  27.2 us (31%)
  waiting for transfers between devices  22.1 us (25%)
  other arithmetic  2.92 us (3%)
  local copies, waits for them, and re-layouts  2.25 us (3%)
    pallas_call x1, Pallas kernels, run_forward(): pl.pallas_call(forward_kernel, out_shape=(jax.ShapeDtypeStruct((T, PX, C)...  15.3 us
    all_to_all x2, starting transfers between devices, shared_with(): lax.all_to_all(jnp.broadcast_to(x[None], (count,) + x.shape), axes, 0, 0)  10.4 us
    all_to_all x2, waiting for transfers between devices, shared_with(): lax.all_to_all(jnp.broadcast_to(x[None], (count,) + x.shape), axes, 0, 0)  9.64 us
    pallas_call x1, Pallas kernels, run_spread(): pl.pallas_call(spread_kernel, out_shape=jax.ShapeDtypeStruct((SLABS, 22 *...  6.52 us
    pallas_call x1, Pallas kernels, run_return(): pl.pallas_call(return_kernel, out_shape=(jax.ShapeDtypeStruct(tile, F32),...  5.67 us
    all_to_all x1, starting transfers between devices, on_device(): mine = lax.all_to_all(mine.reshape(16, HALF // 16, 128), plane, 0, 0)  4.87 us
    ppermute x1, starting transfers between devices, on_device(): mine = (keep + lax.ppermute(send, 'c', swap).astype(F32)).astype(BF16)  4.46 us
    ppermute x1, waiting for transfers between devices, on_device(): prev = lax.ppermute(own, around, to_right)  3.49 us
  transfers between devices with their start and end apart: 9, of which 8 were waited for; matrix products, arithmetic and copies ran while one was open for 2% of the time, Pallas kernels for 17%

profile of v2, /device:TPU:1, one launch (start us, length us, event | category | flops | bytes accessed | tf_op | source)
XLA Modules:
  0.0 86.3 jit_solution(17718812973652163841)
XLA Ops:
  0.6 3.1 %collective-permute-start = (bf16[4,256,192]{2,1,0:T(8,128)(2,1)}, bf16[4,256,192]{2,1,0:T(8,128)(2,1)S(1)}, u32[]{:S(2)}, u32[]{:S(2)}) collective-permute-start(bf16[4,256,192]{2,1,0:T(8,128)(2,1)} %bitcast.14), channel_id=1, source_target_pairs={{0,1},{1,2},{2,3},{3,4},{4,5},{5,6},{6,7},{7,8},{8,9},{9,10},{10,1... | collective-permute-start | bytes 1179656 | tf_op jit(solution)/shard_map/ppermute | solution.py:730
  4.0 2.6 %shard_map.170 = (s32[64]{0:T(128)}, bf16[4,256,256]{2,1,0:T(8,128)(2,1)}, f32[3,392,128]{2,1,0:T(8,128)}, bf16[2,256,768]{2,1,0:T(8,128)(2,1)}, f32[3,1,128]{2,...) custom-call(s32[8,128]{1,0:T(8,128)} %bitcast.17, s32[8,128]{1,0:T(8,128)} %bitcast.18, s32[128]{0:T(128)} %owner_hbm.1, ...), custom_call_target="tpu_custom_call" | custom-call | flops 100000000 | bytes 6000000 | tf_op jit(solution)/shard_map/pallas_call | solution.py:202
  6.7 3.5 %collective-permute-done.prev_hbm = bf16[4,256,192]{2,1,0:T(8,128)(2,1)S(1)} collective-permute-done((bf16[4,256,192]{2,1,0:T(8,128)(2,1)}, bf16[4,256,192]{2,1,0:T(8,128)(2,1)S(1)}, u32[]{:S(2)}, u32[]{:S(2)}) %collective-permute-start) | collective-permute-done | bytes 393248 | tf_op jit(solution)/shard_map/ppermute | solution.py:730
  10.2 2.7 %collective-permute-done.1.next_hbm = bf16[4,256,192]{2,1,0:T(8,128)(2,1)S(1)} collective-permute-done((bf16[4,256,192]{2,1,0:T(8,128)(2,1)}, bf16[4,256,192]{2,1,0:T(8,128)(2,1)S(1)}, u32[]{:S(2)}, u32[]{:S(2)}) %collective-permute-start.1) | collective-permute-done | bytes 393248 | tf_op jit(solution)/shard_map/ppermute | solution.py:731
  12.9 0.8 copy-done.2
  13.6 15.3 %shard_map.171 = (bf16[4,256,192]{2,1,0:T(8,128)(2,1)}, f32[6,512,128]{2,1,0:T(8,128)}, bf16[1280,128]{1,0:T(8,128)(2,1)}, f32[1280,128]{1,0:T(8,128)}) custom-call(s32[64]{0:T(128)} %get-tuple-element.39.where_hbm.where_ref, bf16[4,256,192]{2,1,0:T(8,128)(2,1)} %copy-done.1, bf16[4,256,192]{2,1,0:T(8,128)(2,1)} %copy-done.2, ...), custom_call_target="tpu_custom_call" | custom-call | flops 4000000000 | bytes 8000000 | tf_op jit(solution)/shard_map/pallas_call | solution.py:510
  28.9 4.5 %collective-permute-start.2 = (bf16[1280,128]{1,0:T(8,128)(2,1)}, bf16[1280,128]{1,0:T(8,128)(2,1)S(1)}, u32[]{:S(2)}, u32[]{:S(2)}) collective-permute-start(bf16[1280,128]{1,0:T(8,128)(2,1)} %get-tuple-element.49), channel_id=1, source_target_pairs={{0,1},{1,0},{2,3},{3,2},{4,5},{5,4},{6,7},{7,6},{8,9},{9,8},{10,11... | collective-permute-start | bytes 983048 | tf_op jit(solution)/shard_map/ppermute | solution.py:746
  33.4 1.5 %collective-permute-done.2 = bf16[1280,128]{1,0:T(8,128)(2,1)S(1)} collective-permute-done((bf16[1280,128]{1,0:T(8,128)(2,1)}, bf16[1280,128]{1,0:T(8,128)(2,1)S(1)}, u32[]{:S(2)}, u32[]{:S(2)}) %collective-permute-start.2) | collective-permute-done | bytes 327712 | tf_op jit(solution)/shard_map/ppermute | solution.py:746
  34.9 1.9 %add_convert_fusion.1 = bf16[1280,128]{1,0:T(8,128)(2,1)} fusion(f32[1280,128]{1,0:T(8,128)} %get-tuple-element.48, bf16[1280,128]{1,0:T(8,128)(2,1)S(1)} %collective-permute-done.2), kind=kLoop, calls=%fused_computation.1 | loop fusion | flops 491520 | bytes 1310720 | tf_op jit(solution)/shard_map/convert_element_type | solution.py:746
  36.7 4.9 %all-to-all-start = ((bf16[16,80,128]{2,1,0:T(8,128)(2,1)}), bf16[16,80,128]{2,1,0:T(8,128)(2,1)S(1)}, u32[]{:S(2)}, u32[]{:S(2)}) async-start(bf16[16,80,128]{2,1,0:T(8,128)(2,1)} %bitcast.6), calls=%async_computation | async-start | bytes 655360 | tf_op jit(solution)/shard_map/all_to_all | solution.py:748
  41.6 6.5 %shard_map.172.dpad = f32[6,528,128]{2,1,0:T(8,128)} custom-call(f32[6,512,128]{2,1,0:T(8,128)} %get-tuple-element.50.dmix, f32[3,392,128]{2,1,0:T(8,128)} %get-tuple-element.42.kern_hbm.kern), custom_call_target="tpu_custom_call" | custom-call | flops 1000000000 | bytes 5000000 | tf_op jit(solution)/shard_map/pallas_call | solution.py:572
  48.1 1.2 %all-to-all-done = bf16[16,80,128]{2,1,0:T(8,128)(2,1)S(1)} async-done(((bf16[16,80,128]{2,1,0:T(8,128)(2,1)}), bf16[16,80,128]{2,1,0:T(8,128)(2,1)S(1)}, u32[]{:S(2)}, u32[]{:S(2)}) %all-to-all-start) | async-done | bytes 327712 | tf_op jit(solution)/shard_map/all_to_all | solution.py:748
  49.4 0.7 broadcast_in_dim.4
  50.1 6.2 %all-to-all-start.1 = ((bf16[8,80,128]{2,1,0:T(8,128)(2,1)}), bf16[8,80,128]{2,1,0:T(8,128)(2,1)S(1)}, u32[]{:S(2)}, u32[]{:S(2)}) async-start(bf16[8,80,128]{2,1,0:T(8,128)(2,1)} %broadcast_in_dim.4), calls=%async_computation.1 | async-start | bytes 327680 | tf_op jit(solution)/shard_map/all_to_all | solution.py:703
  56.3 5.7 %shard_map.173 = (f32[4,256,192]{2,1,0:T(8,128)}, bf16[4,256,192]{2,1,0:T(8,128)(2,1)}, bf16[4,256,192]{2,1,0:T(8,128)(2,1)}) custom-call(s32[64]{0:T(128)} %get-tuple-element.39.where_hbm.where_ref, f32[6,528,128]{2,1,0:T(8,128)} %shard_map.172.dpad, bf16[4,256,192]{2,1,0:T(8,128)(2,1)} %bitcast.21), custom_call_target="tpu_custom_call" | custom-call | flops 1000000000 | bytes 5000000 | tf_op jit(solution)/shard_map/pallas_call | solution.py:632
  62.0 2.7 %all-to-all-done.1 = bf16[8,80,128]{2,1,0:T(8,128)(2,1)S(1)} async-done(((bf16[8,80,128]{2,1,0:T(8,128)(2,1)}), bf16[8,80,128]{2,1,0:T(8,128)(2,1)S(1)}, u32[]{:S(2)}, u32[]{:S(2)}) %all-to-all-start.1) | async-done | bytes 163872 | tf_op jit(solution)/shard_map/all_to_all | solution.py:703
  64.6 3.3 %collective-permute-start.3 = (bf16[4,256,192]{2,1,0:T(8,128)(2,1)}, bf16[4,256,192]{2,1,0:T(8,128)(2,1)S(1)}, u32[]{:S(2)}, u32[]{:S(2)}) collective-permute-start(bf16[4,256,192]{2,1,0:T(8,128)(2,1)} %get-tuple-element.60), channel_id=1, source_target_pairs={{1,0},{2,1},{3,2},{4,3},{5,4},{6,5},{7,6},{8,7},{9,8},{10,9},{11,1... | collective-permute-start | bytes 1179656 | tf_op jit(solution)/shard_map/ppermute | solution.py:756
  68.2 0.8 broadcast_in_dim.5
  68.9 4.2 %all-to-all-start.2 = ((bf16[16,80,128]{2,1,0:T(8,128)(2,1)}), bf16[16,80,128]{2,1,0:T(8,128)(2,1)S(1)}, u32[]{:S(2)}, u32[]{:S(2)}) async-start(bf16[16,80,128]{2,1,0:T(8,128)(2,1)} %broadcast_in_dim.5), calls=%async_computation.2 | async-start | bytes 655360 | tf_op jit(solution)/shard_map/all_to_all | solution.py:703
  73.2 2.3 %collective-permute-done.3 = bf16[4,256,192]{2,1,0:T(8,128)(2,1)S(1)} collective-permute-done((bf16[4,256,192]{2,1,0:T(8,128)(2,1)}, bf16[4,256,192]{2,1,0:T(8,128)(2,1)S(1)}, u32[]{:S(2)}, u32[]{:S(2)}) %collective-permute-start.3) | collective-permute-done | bytes 393248 | tf_op jit(solution)/shard_map/ppermute | solution.py:756
  75.5 1.0 %add_convert_fusion = bf16[4,256,192]{2,1,0:T(8,128)(2,1)} fusion(bf16[4,256,192]{2,1,0:T(8,128)(2,1)S(1)} %collective-permute-done.4, f32[4,256,192]{2,1,0:T(8,128)S(1)} %copy-done, bf16[4,256,192]{2,1,0:T(8,128)(2,1)S(1)} %collective-permute-done.3), kind=kLoop, calls=%fused_computation | loop fusion | flops 983040 | bytes 1966080 | tf_op jit(solution)/shard_map/convert_element_type | solution.py:760
  76.5 6.9 %all-to-all-done.2 = bf16[16,80,128]{2,1,0:T(8,128)(2,1)S(1)} async-done(((bf16[16,80,128]{2,1,0:T(8,128)(2,1)}), bf16[16,80,128]{2,1,0:T(8,128)(2,1)S(1)}, u32[]{:S(2)}, u32[]{:S(2)}) %all-to-all-start.2) | async-done | bytes 327712 | tf_op jit(solution)/shard_map/all_to_all | solution.py:703
  84.0 1.3 %collective-permute-done.5.other_ref = bf16[1280,128]{1,0:T(8,128)(2,1)S(1)} collective-permute-done((bf16[1280,128]{1,0:T(8,128)(2,1)S(1)}, bf16[1280,128]{1,0:T(8,128)(2,1)S(1)}, u32[]{:S(2)}, u32[]{:S(2)}) %collective-permute-start.5) | collective-permute-done | bytes 327712 | tf_op jit(solution)/shard_map/ppermute | solution.py:763
  85.2 1.1 %shard_map.174 = (f32[192,768]{1,0:T(8,128)}, f32[192,768]{1,0:T(8,128)}, f32[7,7,192]{2,1,0:T(8,128)}, f32[192]{0:T(256)}, f32[192]{0:T(256)}, /*index=5*/f32[768]{0:T(1024)}) custom-call(s32[1]{0:T(128)} %bitcast.8.core_ref, bf16[1280,128]{1,0:T(8,128)(2,1)S(1)} %bitcast.12, bf16[1280,128]{1,0:T(8,128)(2,1)S(1)} %collective-permute-done.5.other_ref), custom_call_target="tpu_custom_call" | custom-call | flops 1000000 | bytes 2000000 | tf_op jit(solution)/shard_map/pallas_call | solution.py:684
  (11 shorter events, 1.1 us)
Async XLA Ops:
  0.6 9.5 %collective-permute-start = (bf16[4,256,192]{2,1,0:T(8,128)(2,1)}, bf16[4,256,192]{2,1,0:T(8,128)(2,1)S(1)}, u32[]{:S(2)}, u32[]{:S(2)}) collective-permute-start(bf16[4,256,192]{2,1,0:T(8,128)(2,1)} %bitcast.14), channel_id=1, source_target_pairs={{0,1},{1,2},{2,3},{3,4},{4,5},{5,6},{6,7},{7,8},{8,9},{9,10},{10,1... | collective-permute-start | bytes 1179656 | tf_op jit(solution)/shard_map/ppermute | solution.py:730
  3.7 9.1 %collective-permute-start.1 = (bf16[4,256,192]{2,1,0:T(8,128)(2,1)}, bf16[4,256,192]{2,1,0:T(8,128)(2,1)S(1)}, u32[]{:S(2)}, u32[]{:S(2)}) collective-permute-start(bf16[4,256,192]{2,1,0:T(8,128)(2,1)} %bitcast.15), channel_id=1, source_target_pairs={{1,0},{2,1},{3,2},{4,3},{5,4},{6,5},{7,6},{8,7},{9,8},{10,9},{11,1... | collective-permute-start | bytes 1179656 | tf_op jit(solution)/shard_map/ppermute | solution.py:731
  10.2 2.7 %copy-start.1 = (bf16[4,256,192]{2,1,0:T(8,128)(2,1)}, bf16[4,256,192]{2,1,0:T(8,128)(2,1)S(1)}, u32[]{:S(2)}) copy-start(bf16[4,256,192]{2,1,0:T(8,128)(2,1)S(1)} %collective-permute-done.prev_hbm) | copy-start | bytes 1179652
  12.9 0.8 copy-start.2
  28.9 5.9 %collective-permute-start.2 = (bf16[1280,128]{1,0:T(8,128)(2,1)}, bf16[1280,128]{1,0:T(8,128)(2,1)S(1)}, u32[]{:S(2)}, u32[]{:S(2)}) collective-permute-start(bf16[1280,128]{1,0:T(8,128)(2,1)} %get-tuple-element.49), channel_id=1, source_target_pairs={{0,1},{1,0},{2,3},{3,2},{4,5},{5,4},{6,7},{7,6},{8,9},{9,8},{10,11... | collective-permute-start | bytes 983048 | tf_op jit(solution)/shard_map/ppermute | solution.py:746
  36.7 12.6 %all-to-all-start = ((bf16[16,80,128]{2,1,0:T(8,128)(2,1)}), bf16[16,80,128]{2,1,0:T(8,128)(2,1)S(1)}, u32[]{:S(2)}, u32[]{:S(2)}) async-start(bf16[16,80,128]{2,1,0:T(8,128)(2,1)} %bitcast.6), calls=%async_computation | async-start | bytes 655360 | tf_op jit(solution)/shard_map/all_to_all | solution.py:748
  50.1 14.6 %all-to-all-start.1 = ((bf16[8,80,128]{2,1,0:T(8,128)(2,1)}), bf16[8,80,128]{2,1,0:T(8,128)(2,1)S(1)}, u32[]{:S(2)}, u32[]{:S(2)}) async-start(bf16[8,80,128]{2,1,0:T(8,128)(2,1)} %broadcast_in_dim.4), calls=%async_computation.1 | async-start | bytes 327680 | tf_op jit(solution)/shard_map/all_to_all | solution.py:703
  61.9 13.6 %copy-start = (f32[4,256,192]{2,1,0:T(8,128)S(1)}, f32[4,256,192]{2,1,0:T(8,128)}, u32[]{:S(2)}) copy-start(f32[4,256,192]{2,1,0:T(8,128)} %get-tuple-element.59) | copy-start | bytes 2359300
  64.6 10.9 %collective-permute-start.3 = (bf16[4,256,192]{2,1,0:T(8,128)(2,1)}, bf16[4,256,192]{2,1,0:T(8,128)(2,1)S(1)}, u32[]{:S(2)}, u32[]{:S(2)}) collective-permute-start(bf16[4,256,192]{2,1,0:T(8,128)(2,1)} %get-tuple-element.60), channel_id=1, source_target_pairs={{1,0},{2,1},{3,2},{4,3},{5,4},{6,5},{7,6},{8,7},{9,8},{10,9},{11,1... | collective-permute-start | bytes 1179656 | tf_op jit(solution)/shard_map/ppermute | solution.py:756
  68.0 7.5 %collective-permute-start.4 = (bf16[4,256,192]{2,1,0:T(8,128)(2,1)}, bf16[4,256,192]{2,1,0:T(8,128)(2,1)S(1)}, u32[]{:S(2)}, u32[]{:S(2)}) collective-permute-start(bf16[4,256,192]{2,1,0:T(8,128)(2,1)} %get-tuple-element.61), channel_id=1, source_target_pairs={{0,1},{1,2},{2,3},{3,4},{4,5},{5,6},{6,7},{7,8},{8,9},{9,10},{10,1... | collective-permute-start | bytes 1179656 | tf_op jit(solution)/shard_map/ppermute | solution.py:757
  68.9 14.5 %all-to-all-start.2 = ((bf16[16,80,128]{2,1,0:T(8,128)(2,1)}), bf16[16,80,128]{2,1,0:T(8,128)(2,1)S(1)}, u32[]{:S(2)}, u32[]{:S(2)}) async-start(bf16[16,80,128]{2,1,0:T(8,128)(2,1)} %broadcast_in_dim.5), calls=%async_computation.2 | async-start | bytes 655360 | tf_op jit(solution)/shard_map/all_to_all | solution.py:703
  83.4 1.8 %collective-permute-start.5 = (bf16[1280,128]{1,0:T(8,128)(2,1)S(1)}, bf16[1280,128]{1,0:T(8,128)(2,1)S(1)}, u32[]{:S(2)}, u32[]{:S(2)}) collective-permute-start(bf16[1280,128]{1,0:T(8,128)(2,1)S(1)} %bitcast.11), channel_id=1, source_target_pairs={{0,1},{1,0},{2,3},{3,2},{4,5},{5,4},{6,7},{7,6},{8,9},{9,8},{10,11... | collective-permute-start | bytes 983048 | tf_op jit(solution)/shard_map/ppermute | solution.py:763

commit v3 on v2

--- a/solution.py
+++ b/solution.py
@@ -22,7 +22,6 @@
 ROWS = 2560
 HALF = ROWS // 2
 MIB = 1024 * 1024
-VMEM_LIMIT = 60 * MIB
 SLABS = 3 * T // 2
 BLOCKS = 32
 
@@ -110,61 +109,48 @@
 
 
 def prepare_kernel(
-    near_hbm,
-    rot_hbm,
-    owner_hbm,
+    table_ref,
+    vector_ref,
     own_hbm,
+    cot_hbm,
     up_hbm,
+    down_hbm,
     kernel_hbm,
-    gain_hbm,
-    bias_hbm,
-    up_bias_hbm,
     where_ref,
     own_ref,
+    cot_ref,
+    up_ref,
+    down_ref,
     kern,
-    up_ref,
     gain_ref,
     bias_ref,
     up_bias_ref,
-    near_ref,
-    rot_ref,
-    owner_ref,
+    ids,
     own_raw,
-    up_raw,
     kernel_ref,
-    gain_in,
-    bias_in,
-    up_bias_in,
-    ids,
     sems,
 ):
     copies = [
         pltpu.make_async_copy(a, b, sems.at[k])
         for k, (a, b) in enumerate(
             (
-                (near_hbm, near_ref),
-                (rot_hbm, rot_ref),
-                (owner_hbm, owner_ref),
+                (kernel_hbm, kernel_ref),
                 (own_hbm, own_raw),
-                (up_hbm, up_raw),
-                (kernel_hbm, kernel_ref),
-                (gain_hbm, gain_in),
-                (bias_hbm, bias_in),
-                (up_bias_hbm, up_bias_in),
+                (up_hbm, up_ref),
+                (cot_hbm, cot_ref),
+                (down_hbm, down_ref),
             )
         )
     ]
     for copy in copies:
         copy.start()
-    for copy in copies:
-        copy.wait()
 
     position = (lax.axis_index("xh") * 8 + lax.axis_index("z")) * 2 + lax.axis_index("c")
     first = position * T
 
     @pl.loop(0, 128, unroll=8)
     def _(q):
-        at = owner_ref[q] - first
+        at = table_ref[16, q] - first
 
         @pl.when((at >= 0) & (at < T))
         def _():
@@ -172,91 +158,82 @@
 
     for tile in range(T):
         for slot in range(8):
-            row = owner_ref[near_ref[slot, ids[tile]]]
+            row = table_ref[16, table_ref[slot, ids[tile]]]
             block = lax.rem(row // T - position + 1 + BLOCKS, BLOCKS)
             where_ref[tile * 8 + slot] = block * T + lax.rem(row, T)
-            where_ref[T * 8 + tile * 8 + slot] = rot_ref[slot, ids[tile]]
-
-    own_ref[:, :, :C] = own_raw[...]
+            where_ref[T * 8 + tile * 8 + slot] = table_ref[8 + slot, ids[tile]]
+
     own_ref[:, :, C:] = jnp.zeros((T, PX, 256 - C), BF16)
-    for part, value in enumerate(packed_slabs(gain_in[...].reshape(1, C))):
+    for part, value in enumerate(packed_slabs(vector_ref[:, :C])):
         gain_ref[part] = value
-    for part, value in enumerate(packed_slabs(bias_in[...].reshape(1, C))):
+    for part, value in enumerate(packed_slabs(vector_ref[:, 256 : 256 + C])):
         bias_ref[part] = value
-    up_bias_ref[...] = up_bias_in[...].reshape(1, HID)
+    up_bias_ref[...] = vector_ref[:, 512:]
+    copies[0].wait()
     for a in range(7):
         for part, value in enumerate(packed_slabs(kernel_ref[a])):
-            for b in range(7):
-                tap = jnp.broadcast_to(value[b : b + 1], (8, 128))
-                kern[part, 8 * (a * 7 + b) : 8 * (a * 7 + b + 1), :] = tap
-    up_ref[0, :C, :] = up_raw[...]
-    up_ref[0, C:, :] = jnp.zeros((64, HID), BF16)
-    up_ref[1, :64, :] = jnp.zeros((64, HID), BF16)
-    up_ref[1, 64:, :] = up_raw[...]
+            kern[part, 8 * a : 8 * a + 7, :] = value
+    copies[1].wait()
+    own_ref[:, :, :C] = own_raw[...]
+    for copy in copies[2:]:
+        copy.wait()
 
 
 def run_prepare(*args):
     vmem = pl.BlockSpec(memory_space=pltpu.VMEM)
     smem = pl.BlockSpec(memory_space=pltpu.SMEM)
-    hbm = pl.BlockSpec(memory_space=pltpu.HBM)
     return pl.pallas_call(
         prepare_kernel,
         out_shape=(
             jax.ShapeDtypeStruct((T * 16,), jnp.int32),
             jax.ShapeDtypeStruct((T, PX, 256), BF16),
-            jax.ShapeDtypeStruct((3, 8 * 49, 128), F32),
-            jax.ShapeDtypeStruct((2, 256, HID), BF16),
+            jax.ShapeDtypeStruct((T, PX, C), BF16),
+            jax.ShapeDtypeStruct((C, HID), BF16),
+            jax.ShapeDtypeStruct((C, HID), BF16),
+            jax.ShapeDtypeStruct((3, 56, 128), F32),
             jax.ShapeDtypeStruct((3, 1, 128), F32),
             jax.ShapeDtypeStruct((3, 1, 128), F32),
             jax.ShapeDtypeStruct((1, HID), F32),
         ),
-        in_specs=[hbm] * 9,
-        out_specs=(smem,) + (vmem,) * 6,
+        in_specs=[smem, vmem] + [pl.BlockSpec(memory_space=pl.ANY)] * 5,
+        out_specs=(smem,) + (vmem,) * 8,
         scratch_shapes=[
-            pltpu.SMEM((8, 128), jnp.int32),
-            pltpu.SMEM((8, 128), jnp.int32),
-            pltpu.SMEM((128,), jnp.int32),
+            pltpu.SMEM((T,), jnp.int32),
             pltpu.VMEM((T, PX, C), BF16),
-            pltpu.VMEM((C, HID), BF16),
             pltpu.VMEM((7, 7, C), F32),
-            pltpu.VMEM((C,), F32),
-            pltpu.VMEM((C,), F32),
-            pltpu.VMEM((HID,), F32),
-            pltpu.SMEM((T,), jnp.int32),
-            pltpu.SemaphoreType.DMA((9,)),
+            pltpu.SemaphoreType.DMA((5,)),
         ],
-        compiler_params=pltpu.CompilerParams(vmem_limit_bytes=VMEM_LIMIT),
+        compiler_params=pltpu.CompilerParams(vmem_limit_bytes=52736 * 1024),
         cost_estimate=pl.CostEstimate(flops=10**8, bytes_accessed=6 * 10**6, transcendentals=0),
     )(*args)
 
 
+def repeat_taps(taps_ref, kern):
+    for part in range(3):
+        for a in range(7):
+            for b in range(7):
+                at = 8 * (a * 7 + b)
+                tap = taps_ref[part, 8 * a + b : 8 * a + b + 1, :]
+                kern[part, at : at + 8, :] = jnp.broadcast_to(tap, (8, 128))
+
+
 def forward_kernel(
-    where_hbm,
-    prev_hbm,
-    next_hbm,
-    own_hbm,
-    cot_hbm,
-    down_hbm,
-    up_hbm,
-    kern_hbm,
-    gain_hbm,
-    bias_hbm,
-    up_bias_hbm,
-    updated_hbm,
-    dmix_hbm,
-    send_ref,
-    keep_ref,
     where_ref,
-    raw,
+    prev_ref,
+    next_ref,
+    own_ref,
     cot_ref,
+    up_raw,
     down_ref,
-    up_ref,
-    kern,
+    taps_ref,
     gain_ref,
     bias_ref,
     up_bias_ref,
+    updated_hbm,
+    dmix,
+    send_ref,
+    keep_ref,
     out_ref,
-    dmix,
     src,
     pad,
     mix,
@@ -270,41 +247,26 @@
     back_ref32,
     act_ref,
     d_up_ref,
-    sems,
+    up_ref,
+    kern,
+    sem,
 ):
     low_half = lane_is_low()
     core = lax.axis_index("c")
-    copies = [
-        pltpu.make_async_copy(a, b, sems.at[k])
-        for k, (a, b) in enumerate(
-            (
-                (where_hbm, where_ref),
-                (prev_hbm, raw.at[0:T]),
-                (next_hbm, raw.at[T:]),
-                (own_hbm, src.at[T : 2 * T]),
-                (kern_hbm, kern),
-                (gain_hbm, gain_ref),
-                (bias_hbm, bias_ref),
-                (up_hbm, up_ref),
-                (down_hbm, down_ref),
-                (cot_hbm, cot_ref),
-                (up_bias_hbm, up_bias_ref),
-            )
-        )
-    ]
-    for copy in copies:
-        copy.start()
     src[0:T, :, C:] = jnp.zeros((T, PX, 256 - C), BF16)
     src[2 * T :, :, C:] = jnp.zeros((T, PX, 256 - C), BF16)
+    src[0:T, :, :C] = prev_ref[...]
+    src[T : 2 * T] = own_ref[...]
+    up_ref[0, :C, :] = up_raw[...]
+    up_ref[0, C:, :] = jnp.zeros((64, HID), BF16)
+    up_ref[1, :64, :] = jnp.zeros((64, HID), BF16)
+    up_ref[1, 64:, :] = up_raw[...]
+    repeat_taps(taps_ref, kern)
+    src[2 * T :, :, :C] = next_ref[...]
     g_up_bias[...] = jnp.zeros_like(g_up_bias)
     g_small[...] = jnp.zeros_like(g_small)
     dmix[...] = jnp.zeros_like(dmix)
     grads_ref[...] = jnp.zeros_like(grads_ref)
-    for copy in copies[:4]:
-        copy.wait()
-    src[0:T, :, :C] = raw[0:T]
-    src[2 * T :, :, :C] = raw[T:]
-
     def put_rows(pair, half, start, count, value):
         rows = pl.ds(start, count)
         if half == 0:
@@ -345,9 +307,6 @@
                 for i in range(S):
                     put_rows(pair, half, (i + 3) * W + 8 * block, 8, total[8 * i : 8 * i + 8])
 
-    for copy in copies[4:7]:
-        copy.wait()
-
     @pl.loop(0, 3 * T // 2)
     def _(slab):
         part = lax.rem(slab, 3)
@@ -390,50 +349,59 @@
                 standard * gain_ref[k] + bias_ref[k]
             ).astype(BF16)
 
-    for copy in copies[7:]:
-        copy.wait()
-
-    @pl.loop(0, T // 2)
+    def enter(step, half, chunk, x, cot):
+        hid = slice(256 * chunk, 256 * (chunk + 1))
+        up_ref32[step % 3] = jnp.dot(x, up_ref[half, :, hid], preferred_element_type=F32)
+        back_ref32[step % 3] = jnp.dot(cot, down_ref[:, hid], preferred_element_type=F32)
+
+    @pl.loop(0, T // 2, unroll=2)
     def _(pair):
-        normed_grads = []
-        for half in range(2):
-            tile = pair * 2 + half
-            x = normed[pair, :, 128 * half : 128 * half + 256]
-            x_t = jnp.transpose(x.astype(F32)).astype(BF16)
-            cot = cot_ref[tile]
-            cot_t = jnp.transpose(cot.astype(F32)).astype(BF16)
-            branch = jnp.zeros((PX, C), F32)
-            normed_grad = jnp.zeros((PX, 256), F32)
-            for chunk in range(3):
-                hid = slice(256 * chunk, 256 * (chunk + 1))
-                up_ref32[...] = jnp.dot(x, up_ref[half, :, hid], preferred_element_type=F32)
-                back_ref32[...] = jnp.dot(cot, down_ref[:, hid], preferred_element_type=F32)
-                bias_sum = jnp.zeros((8, 256), F32)
-                for r in range(0, PX, 16):
-                    rows = slice(r, r + 16)
-                    value, slope = gelu_pair(up_ref32[rows, :] + up_bias_ref[:, hid])
-                    d_up = back_ref32[rows, :] * slope
-                    bias_sum += d_up[:8] + d_up[8:]
-                    act_ref[rows, :] = value.astype(BF16)
-                    d_up_ref[rows, :] = d_up.astype(BF16)
-                g_up_bias[:, hid] += bias_sum
-                activation = act_ref[...]
-                d_up_b = d_up_ref[...]
-                branch += times_transposed(activation, down_ref[:, hid])
-                down_grad = jnp.dot(cot_t, activation, preferred_element_type=F32)
-                up_grad = jnp.dot(x_t, d_up_b, preferred_element_type=F32)
-                for k in range(2):
-                    at = C * (2 * chunk + k)
-                    lanes = slice(128 * k, 128 * (k + 1))
-                    grads_ref[at : at + C, :] += up_grad[64 * half : 64 * half + C, lanes]
-                    at += WEIGHT_ROWS // 2
-                    grads_ref[at : at + C, :] += down_grad[:, lanes]
-                normed_grad += times_transposed(d_up_b, up_ref[half, :, hid])
-            out_ref[tile] = (src[T + tile, :, :C].astype(F32) + branch).astype(BF16)
-            normed_grads.append(normed_grad)
-        mix[pair * 3] = normed_grads[0][:, :128]
-        mix[pair * 3 + 1] = normed_grads[0][:, 128:] + normed_grads[1][:, :128]
-        mix[pair * 3 + 2] = normed_grads[1][:, 128:]
+        xs = [normed[pair, :, 128 * half : 128 * half + 256] for half in range(2)]
+        cots = [cot_ref[pair * 2 + half] for half in range(2)]
+        steps = [(half, chunk) for half in range(2) for chunk in range(3)]
+        enter(0, 0, 0, xs[0], cots[0])
+        for step, (half, chunk) in enumerate(steps):
+            if step + 1 < len(steps):
+                after = steps[step + 1]
+                enter(step + 1, *after, xs[after[0]], cots[after[0]])
+            hid = slice(256 * chunk, 256 * (chunk + 1))
+            if chunk == 0:
+                x_t = jnp.transpose(xs[half].astype(F32)).astype(BF16)
+                cot_t = jnp.transpose(cots[half].astype(F32)).astype(BF16)
+                branch = jnp.zeros((PX, C), F32)
+                normed_grad = jnp.zeros((PX, 256), F32)
+            slot = step % 3
+            bias_sum = jnp.zeros((8, 256), F32)
+            for r in range(0, PX, 16):
+                rows = slice(r, r + 16)
+                value, slope = gelu_pair(up_ref32[slot, rows, :] + up_bias_ref[:, hid])
+                d_up = back_ref32[slot, rows, :] * slope
+                bias_sum += d_up[:8] + d_up[8:]
+                act_ref[slot, rows, :] = value.astype(BF16)
+                d_up_ref[slot, rows, :] = d_up.astype(BF16)
+            g_up_bias[:, hid] += bias_sum
+            activation = act_ref[slot]
+            d_up_b = d_up_ref[slot]
+            branch += times_transposed(activation, down_ref[:, hid])
+            down_grad = jnp.dot(cot_t, activation, preferred_element_type=F32)
+            up_grad = jnp.dot(x_t, d_up_b, preferred_element_type=F32)
+            for k in range(2):
+                at = C * (2 * chunk + k)
+                lanes = slice(128 * k, 128 * (k + 1))
+                grads_ref[at : at + C, :] += up_grad[64 * half : 64 * half + C, lanes]
+                at += WEIGHT_ROWS // 2
+                grads_ref[at : at + C, :] += down_grad[:, lanes]
+            normed_grad += times_transposed(d_up_b, up_ref[half, :, hid])
+            if chunk == 2:
+                tile = pair * 2 + half
+                own = src[T + tile, :, :C].astype(F32)
+                out_ref[tile] = (own + branch).astype(BF16)
+                if half == 0:
+                    mix[pair * 3] = normed_grad[:, :128]
+                    mix[pair * 3 + 1] = normed_grad[:, 128:]
+                else:
+                    mix[pair * 3 + 1] += normed_grad[:, :128]
+                    mix[pair * 3 + 2] = normed_grad[:, 128:]
 
     @pl.loop(0, (T // 2) * (PX // CH), unroll=4)
     def _(step):
@@ -458,12 +426,8 @@
                 at = (start // S + r) * DW + 8
                 dmix[pair * 3 + k, pl.ds(pl.multiple_of(at, 8), S), :] = d_mixed[r * S : (r + 1) * S]
 
-    results = [
-        pltpu.make_async_copy(out_ref, updated_hbm, sems.at[11]),
-        pltpu.make_async_copy(dmix, dmix_hbm, sems.at[12]),
-    ]
-    for result in results:
-        result.start()
+    result = pltpu.make_async_copy(out_ref, updated_hbm, sem)
+    result.start()
 
     @pl.loop(0, 3 * T // 2)
     def _(slab):
@@ -495,8 +459,7 @@
     grads_ref[WEIGHT_ROWS + 112 : WEIGHT_ROWS + 128, :] = bias_rows
     send_ref[...] = grads_ref[pl.ds((1 - core) * HALF, HALF), :].astype(BF16)
     keep_ref[...] = grads_ref[pl.ds(core * HALF, HALF), :]
-    for result in results:
-        result.wait()
+    result.wait()
 
 
 def times_transposed(x, y):
@@ -505,7 +468,7 @@
 
 def run_forward(*args):
     vmem = pl.BlockSpec(memory_space=pltpu.VMEM)
-    hbm = pl.BlockSpec(memory_space=pl.ANY)
+    smem = pl.BlockSpec(memory_space=pltpu.SMEM)
     slab = pltpu.VMEM((SLABS, PX, 128), F32)
     return pl.pallas_call(
         forward_kernel,
@@ -515,20 +478,10 @@
             jax.ShapeDtypeStruct((HALF, 128), BF16),
             jax.ShapeDtypeStruct((HALF, 128), F32),
         ),
-        in_specs=[hbm] * 11,
-        out_specs=(hbm, hbm, vmem, vmem),
+        in_specs=[smem] + [vmem] * 10,
+        out_specs=(pl.BlockSpec(memory_space=pl.ANY), vmem, vmem, vmem),
         scratch_shapes=[
-            pltpu.SMEM((T * 16,), jnp.int32),
-            pltpu.VMEM((2 * T, PX, C), BF16),
             pltpu.VMEM((T, PX, C), BF16),
-            pltpu.VMEM((C, HID), BF16),
-            pltpu.VMEM((2, 256, HID), BF16),
-            pltpu.VMEM((3, 8 * 49, 128), F32),
-            pltpu.VMEM((3, 1, 128), F32),
-            pltpu.VMEM((3, 1, 128), F32),
-            pltpu.VMEM((1, HID), F32),
-            pltpu.VMEM((T, PX, C), BF16),
-            pltpu.VMEM((SLABS, S * DW, 128), F32),
             pltpu.VMEM((3 * T, PX, 256), BF16),
             pltpu.VMEM((SLABS, 22 * W, 128), F32),
             slab,
@@ -538,18 +491,22 @@
             pltpu.VMEM((8, HID), F32),
             pltpu.VMEM((3, 8 * 56, 128), F32),
             pltpu.VMEM((ROWS, 128), F32),
-            pltpu.VMEM((PX, 256), F32),
-            pltpu.VMEM((PX, 256), F32),
-            pltpu.VMEM((PX, 256), BF16),
-            pltpu.VMEM((PX, 256), BF16),
-            pltpu.SemaphoreType.DMA((13,)),
+            pltpu.VMEM((3, PX, 256), F32),
+            pltpu.VMEM((3, PX, 256), F32),
+            pltpu.VMEM((3, PX, 256), BF16),
+            pltpu.VMEM((3, PX, 256), BF16),
+            pltpu.VMEM((2, 256, HID), BF16),
+            pltpu.VMEM((3, 8 * 49, 128), F32),
+            pltpu.SemaphoreType.DMA,
         ],
-        compiler_params=pltpu.CompilerParams(vmem_limit_bytes=55 * MIB),
+        compiler_params=pltpu.CompilerParams(vmem_limit_bytes=24 * MIB),
         cost_estimate=pl.CostEstimate(flops=4 * 10**9, bytes_accessed=8 * 10**6, transcendentals=10**6),
     )(*args)
 
 
-def spread_kernel(dmix, kern, dpad):
+def spread_kernel(dmix, taps_ref, dpad, kern):
+    repeat_taps(taps_ref, kern)
+
     @pl.loop(0, SLABS)
     def _(slab):
         part = lax.rem(slab, 3)
@@ -574,16 +531,13 @@
         out_shape=jax.ShapeDtypeStruct((SLABS, 22 * W, 128), F32),
         in_specs=[vmem] * 2,
         out_specs=vmem,
-        compiler_params=pltpu.CompilerParams(vmem_limit_bytes=VMEM_LIMIT),
+        scratch_shapes=[pltpu.VMEM((3, 8 * 49, 128), F32)],
+        compiler_params=pltpu.CompilerParams(vmem_limit_bytes=12 * MIB),
         cost_estimate=pl.CostEstimate(flops=10**9, bytes_accessed=5 * 10**6, transcendentals=0),
     )(dmix, taps)
 
 
-def return_kernel(
-    where_ref, dpad, cot_hbm, part_ref, to_prev_ref, to_next_ref, collected, cot_ref, sem
-):
-    copy = pltpu.make_async_copy(cot_hbm, cot_ref, sem)
-    copy.start()
+def return_kernel(where_ref, dpad, cot_ref, part_ref, to_prev_ref, to_next_ref, collected):
     collected[...] = jnp.zeros_like(collected)
 
     @pl.loop(0, T // 2)
@@ -604,7 +558,6 @@
 
     to_prev_ref[...] = collected[0:T, :, :C].astype(BF16)
     to_next_ref[...] = collected[2 * T :, :, :C].astype(BF16)
-    copy.wait()
 
     @pl.loop(0, T // 2)
     def _(pair):
@@ -636,14 +589,10 @@
             jax.ShapeDtypeStruct(tile, BF16),
             jax.ShapeDtypeStruct(tile, BF16),
         ),
-        in_specs=[smem, vmem, pl.BlockSpec(memory_space=pltpu.HBM)],
+        in_specs=[smem, vmem, vmem],
         out_specs=(vmem,) * 3,
-        scratch_shapes=[
-            pltpu.VMEM((3 * T, PX, 256), F32),
-            pltpu.VMEM((T, PX, C), BF16),
-            pltpu.SemaphoreType.DMA,
-        ],
-        compiler_params=pltpu.CompilerParams(vmem_limit_bytes=VMEM_LIMIT),
+        scratch_shapes=[pltpu.VMEM((3 * T, PX, 256), F32)],
+        compiler_params=pltpu.CompilerParams(vmem_limit_bytes=16 * MIB),
         cost_estimate=pl.CostEstimate(flops=10**9, bytes_accessed=5 * 10**6, transcendentals=0),
     )(where, dpad, cot)
 
@@ -729,19 +678,15 @@
     cot = cotangent.reshape(T, PX, C)
     prev = lax.ppermute(own, around, to_right)
     nxt = lax.ppermute(own, around, to_left)
-    where, wide, taps, up, gain, bias, up_bias = run_prepare(
-        neighbours.T,
-        rotation.T,
-        tile_owner,
-        own,
-        up_weight,
-        depth_kernel,
-        layer_norm_gain,
-        layer_norm_bias,
-        up_bias,
+    table = jnp.concatenate([neighbours.T, rotation.T, tile_owner[None]])
+    vector = jnp.concatenate(
+        [jnp.pad(x, (0, 64)) for x in (layer_norm_gain, layer_norm_bias)] + [up_bias]
+    )
+    where, wide, near_cot, up, down_t, taps, gain, bias, up_bias = run_prepare(
+        table, vector[None], own, cot, up_weight, down_weight.T, depth_kernel
     )
     updated, dmix, send, keep = run_forward(
-        where, prev, nxt, wide, cot, down_weight.T, up, taps, gain, bias, up_bias
+        where, prev, nxt, wide, near_cot, up, down_t, taps, gain, bias, up_bias
     )
     mine = (keep + lax.ppermute(send, "c", swap).astype(F32)).astype(BF16)
     dmix, mine = lax.optimization_barrier((dmix, mine))
@@ -751,7 +696,7 @@
     mine = total_of(mine).astype(BF16)
     dpad, mine = lax.optimization_barrier((dpad, mine))
     mine = shared_with(mine, "z", 8)
-    part, to_prev, to_next = run_return(where, dpad, cot)
+    part, to_prev, to_next = run_return(where, dpad, near_cot)
     mine, to_prev, to_next = lax.optimization_barrier((mine, to_prev, to_next))
     from_right = lax.ppermute(to_prev, around, to_left)
     from_left = lax.ppermute(to_next, around, to_right)

time: 86.8 us -> 81.7 us (0.941)
  Pallas kernels: 31.2 us -> 23.5 us
  local copies, waits for them, and re-layouts: 2.25 us -> 6.8 us
  waiting for transfers between devices: 22.1 us -> 20.2 us
    unnamed x6 -> x10, local copies, waits for them, and re-layouts: 0.8 us -> 5.34 us
    ppermute x1, waiting for transfers between devices: 3.49 us -> 0.01 us  [on_device(): prev = lax.ppermute(own, around, to_right)]
    pallas_call x1, Pallas kernels: 15.3 us -> 12.3 us  [run_forward(): pl.pallas_call(forward_kernel, out_shape=(jax.ShapeDtypeStruct((T, PX, C)...]
    pallas_call x1, Pallas kernels: 6.52 us -> 3.88 us  [run_spread(): pl.pallas_call(spread_kernel, out_shape=jax.ShapeDtypeStruct((SLABS, 22 *...]
    pallas_call x1, Pallas kernels: 5.67 us -> 3.58 us  [run_return(): pl.pallas_call(return_kernel, out_shape=(jax.ShapeDtypeStruct(tile, F32),...]
    concatenate x0 -> x2, other arithmetic: none -> 1.45 us  [the longest x1 0.73 us: on_device(): jnp.concatenate([jnp.pad(x, (0, 64)) for x in (layer_norm_gain, layer_nor...]
    all_to_all x1, waiting for transfers between devices: 1.21 us -> 2.66 us  [on_device(): mine = lax.all_to_all(mine.reshape(16, HALF // 16, 128), plane, 0, 0)]
    convert_element_type x1, other arithmetic: 1.88 us -> 0.81 us  [on_device(): mine = (keep + lax.ppermute(send, 'c', swap).astype(F32)).astype(BF16)]
  transfers between devices with their start and end apart: 9 -> 9, of which waited for: 8 -> 7; matrix products, arithmetic and copies ran while one was open for 2% -> 4% of each run, Pallas kernels for 17% -> 12%
where the time goes in v3:
time: 81.7 us; the launch traced here: 81.1 us
  starting transfers between devices  26.5 us (32%)
  Pallas kernels  23.5 us (29%)
  waiting for transfers between devices  20.2 us (25%)
  local copies, waits for them, and re-layouts  6.8 us (8%)
  other arithmetic  3.3 us (4%)
    pallas_call x1, Pallas kernels, run_forward(): pl.pallas_call(forward_kernel, out_shape=(jax.ShapeDtypeStruct((T, PX, C)...  12.3 us
    all_to_all x2, waiting for transfers between devices, shared_with(): lax.all_to_all(jnp.broadcast_to(x[None], (count,) + x.shape), axes, 0, 0)  10.3 us
    all_to_all x2, starting transfers between devices, shared_with(): lax.all_to_all(jnp.broadcast_to(x[None], (count,) + x.shape), axes, 0, 0)  9.88 us
    unnamed x10, local copies, waits for them, and re-layouts  5.34 us
    all_to_all x1, starting transfers between devices, on_device(): mine = lax.all_to_all(mine.reshape(16, HALF // 16, 128), plane, 0, 0)  4.87 us
    ppermute x1, starting transfers between devices, on_device(): mine = (keep + lax.ppermute(send, 'c', swap).astype(F32)).astype(BF16)  4.31 us
    pallas_call x1, Pallas kernels, run_spread(): pl.pallas_call(spread_kernel, out_shape=jax.ShapeDtypeStruct((SLABS, 22 *...  3.88 us
    pallas_call x1, Pallas kernels, run_return(): pl.pallas_call(return_kernel, out_shape=(jax.ShapeDtypeStruct(tile, F32),...  3.58 us
  transfers between devices with their start and end apart: 9, of which 7 were waited for; matrix products, arithmetic and copies ran while one was open for 4% of the time, Pallas kernels for 12%

profile of v3, /device:TPU:1, one launch (start us, length us, event | category | flops | bytes accessed | tf_op | source)
XLA Modules:
  0.0 81.1 jit_solution(14257807846784796275)
XLA Ops:
  0.6 3.1 %collective-permute-start = (bf16[4,256,192]{2,1,0:T(8,128)(2,1)}, bf16[4,256,192]{2,1,0:T(8,128)(2,1)S(1)}, u32[]{:S(2)}, u32[]{:S(2)}) collective-permute-start(bf16[4,256,192]{2,1,0:T(8,128)(2,1)} %bitcast.16), channel_id=1, source_target_pairs={{0,1},{1,2},{2,3},{3,4},{4,5},{5,6},{6,7},{7,8},{8,9},{9,10},{10,1... | collective-permute-start | bytes 1179656 | tf_op jit(solution)/shard_map/ppermute | solution.py:679
  5.5 1.0 %copy-done = bf16[192,768]{1,0:T(8,128)(2,1)S(1)} copy-done((bf16[192,768]{1,0:T(8,128)(2,1)S(1)}, bf16[192,768]{1,0:T(8,128)(2,1)}, u32[]{:S(2)}) %copy-start) | copy-done | bytes 294936
  6.5 1.0 %copy-done.1 = bf16[768,192]{0,1:T(8,128)(2,1)S(1)} copy-done((bf16[768,192]{0,1:T(8,128)(2,1)S(1)}, bf16[768,192]{0,1:T(8,128)(2,1)}, u32[]{:S(2)}) %copy-start.1) | copy-done | bytes 294936
  7.4 0.8 %copy-done.2 = f32[7,7,192]{2,1,0:T(8,128)S(1)} copy-done((f32[7,7,192]{2,1,0:T(8,128)S(1)}, f32[7,7,192]{2,1,0:T(8,128)}, u32[]{:S(2)}) %copy-start.2) | copy-done | bytes 37656
  8.2 2.7 %shard_map.170 = (s32[64]{0:T(128)S(1)}, bf16[4,256,256]{2,1,0:T(8,128)(2,1)S(1)}, bf16[4,256,192]{2,1,0:T(8,128)(2,1)S(1)}, bf16[192,768]{1,0:T(8,128)(2,1)S(1)...) custom-call(s32[17,128]{1,0:T(8,128)S(1)} %pad_add_fusion.table_ref,, ...), custom_call_target="tpu_custom_call" | custom-call | flops 100000000 | bytes 6000000 | tf_op jit(solution)/shard_map/pallas_call | solution.py:185
  10.9 1.9 %collective-permute-done.1.next_ref = bf16[4,256,192]{2,1,0:T(8,128)(2,1)S(1)} collective-permute-done((bf16[4,256,192]{2,1,0:T(8,128)(2,1)}, bf16[4,256,192]{2,1,0:T(8,128)(2,1)S(1)}, u32[]{:S(2)}, u32[]{:S(2)}) %collective-permute-start.1) | collective-permute-done | bytes 393248 | tf_op jit(solution)/shard_map/ppermute | solution.py:680
  12.8 12.3 %shard_map.171 = (bf16[4,256,192]{2,1,0:T(8,128)(2,1)}, f32[6,512,128]{2,1,0:T(8,128)S(1)}, bf16[1280,128]{1,0:T(8,128)(2,1)S(1)}, f32[1280,128]{1,0:T(8,128)S(1)}) custom-call(s32[64]{0:T(128)S(1)} %get-tuple-element.41.where_ref, bf16[4,256,192]{2,1,0:T(8,128)(2,1)S(1)} %collective-permute-done.prev_ref, ...), custom_call_target="tpu_custom_call" | custom-call | flops 4000000000 | bytes 8000000 | tf_op jit(solution)/shard_map/pallas_call | solution.py:473
  25.2 4.3 %collective-permute-start.2 = (bf16[1280,128]{1,0:T(8,128)(2,1)S(1)}, bf16[1280,128]{1,0:T(8,128)(2,1)S(1)}, u32[]{:S(2)}, u32[]{:S(2)}) collective-permute-start(bf16[1280,128]{1,0:T(8,128)(2,1)S(1)} %get-tuple-element.53), channel_id=1, source_target_pairs={{0,1},{1,0},{2,3},{3,2},{4,5},{5,4},{6,7},{7,6},{8,9},{9,8},{10,11... | collective-permute-start | bytes 983048 | tf_op jit(solution)/shard_map/ppermute | solution.py:691
  29.5 1.3 %collective-permute-done.2 = bf16[1280,128]{1,0:T(8,128)(2,1)S(1)} collective-permute-done((bf16[1280,128]{1,0:T(8,128)(2,1)S(1)}, bf16[1280,128]{1,0:T(8,128)(2,1)S(1)}, u32[]{:S(2)}, u32[]{:S(2)}) %collective-permute-start.2) | collective-permute-done | bytes 327712 | tf_op jit(solution)/shard_map/ppermute | solution.py:691
  31.5 4.9 %all-to-all-start = ((bf16[16,80,128]{2,1,0:T(8,128)(2,1)}), bf16[16,80,128]{2,1,0:T(8,128)(2,1)S(1)}, u32[]{:S(2)}, u32[]{:S(2)}) async-start(bf16[16,80,128]{2,1,0:T(8,128)(2,1)} %bitcast.7), calls=%async_computation | async-start | bytes 655360 | tf_op jit(solution)/shard_map/all_to_all | solution.py:693
  36.4 3.9 %shard_map.172.dpad = f32[6,528,128]{2,1,0:T(8,128)S(1)} custom-call(f32[6,512,128]{2,1,0:T(8,128)S(1)} %get-tuple-element.54.dmix, f32[3,56,128]{2,1,0:T(8,128)S(1)} %get-tuple-element.46.taps_ref), custom_call_target="tpu_custom_call" | custom-call | flops 1000000000 | bytes 5000000 | tf_op jit(solution)/shard_map/pallas_call | solution.py:529
  40.3 1.2 %copy-done.3 = f32[6,528,128]{2,1,0:T(8,128)} copy-done((f32[6,528,128]{2,1,0:T(8,128)}, f32[6,528,128]{2,1,0:T(8,128)S(1)}, u32[]{:S(2)}) %copy-start.3) | copy-done | bytes 1622040
  41.5 2.7 %all-to-all-done = bf16[16,80,128]{2,1,0:T(8,128)(2,1)S(1)} async-done(((bf16[16,80,128]{2,1,0:T(8,128)(2,1)}), bf16[16,80,128]{2,1,0:T(8,128)(2,1)S(1)}, u32[]{:S(2)}, u32[]{:S(2)}) %all-to-all-start) | async-done | bytes 327712 | tf_op jit(solution)/shard_map/all_to_all | solution.py:693
  44.9 6.3 %all-to-all-start.1 = ((bf16[8,80,128]{2,1,0:T(8,128)(2,1)}), bf16[8,80,128]{2,1,0:T(8,128)(2,1)S(1)}, u32[]{:S(2)}, u32[]{:S(2)}) async-start(bf16[8,80,128]{2,1,0:T(8,128)(2,1)} %broadcast_in_dim.20), calls=%async_computation.1 | async-start | bytes 327680 | tf_op jit(solution)/shard_map/all_to_all | solution.py:652
  51.2 1.4 %copy-done.4 = f32[6,528,128]{2,1,0:T(8,128)S(1)} copy-done((f32[6,528,128]{2,1,0:T(8,128)S(1)}, f32[6,528,128]{2,1,0:T(8,128)}, u32[]{:S(2)}) %copy-start.4) | copy-done | bytes 1622040
  52.6 3.6 %shard_map.173 = (f32[4,256,192]{2,1,0:T(8,128)S(1)}, bf16[4,256,192]{2,1,0:T(8,128)(2,1)S(1)}, bf16[4,256,192]{2,1,0:T(8,128)(2,1)S(1)}) custom-call(s32[64]{0:T(128)S(1)} %get-tuple-element.41.where_ref, f32[6,528,128]{2,1,0:T(8,128)S(1)} %copy-done.4, bf16[4,256,192]{2,1,0:T(8,128)(2,1)S(1)} %get-tuple-element.43.cot_ref), custom_call_target="tpu_custom_call" | custom-call | flops 1000000000 | bytes 5000000 | tf_op jit(solution)/shard_map/pallas_call | solution.py:585
  56.2 3.4 %all-to-all-done.1 = bf16[8,80,128]{2,1,0:T(8,128)(2,1)S(1)} async-done(((bf16[8,80,128]{2,1,0:T(8,128)(2,1)}), bf16[8,80,128]{2,1,0:T(8,128)(2,1)S(1)}, u32[]{:S(2)}, u32[]{:S(2)}) %all-to-all-start.1) | async-done | bytes 163872 | tf_op jit(solution)/shard_map/all_to_all | solution.py:652
  59.6 3.3 %collective-permute-start.3 = (bf16[4,256,192]{2,1,0:T(8,128)(2,1)S(1)}, bf16[4,256,192]{2,1,0:T(8,128)(2,1)S(1)}, u32[]{:S(2)}, u32[]{:S(2)}) collective-permute-start(bf16[4,256,192]{2,1,0:T(8,128)(2,1)S(1)} %get-tuple-element.64), channel_id=1, source_target_pairs={{1,0},{2,1},{3,2},{4,3},{5,4},{6,5},{7,6},{8,7},{9,8},{10,9},{11,1... | collective-permute-start | bytes 1179656 | tf_op jit(solution)/shard_map/ppermute | solution.py:701
  63.9 3.5 %all-to-all-start.2 = ((bf16[16,80,128]{2,1,0:T(8,128)(2,1)}), bf16[16,80,128]{2,1,0:T(8,128)(2,1)S(1)}, u32[]{:S(2)}, u32[]{:S(2)}) async-start(bf16[16,80,128]{2,1,0:T(8,128)(2,1)} %broadcast_in_dim.21), calls=%async_computation.2 | async-start | bytes 655360 | tf_op jit(solution)/shard_map/all_to_all | solution.py:652
  67.5 2.8 %collective-permute-done.3 = bf16[4,256,192]{2,1,0:T(8,128)(2,1)S(1)} collective-permute-done((bf16[4,256,192]{2,1,0:T(8,128)(2,1)S(1)}, bf16[4,256,192]{2,1,0:T(8,128)(2,1)S(1)}, u32[]{:S(2)}, u32[]{:S(2)}) %collective-permute-start.3) | collective-permute-done | bytes 393248 | tf_op jit(solution)/shard_map/ppermute | solution.py:701
  70.3 1.0 %add_convert_fusion = bf16[4,256,192]{2,1,0:T(8,128)(2,1)} fusion(bf16[4,256,192]{2,1,0:T(8,128)(2,1)S(1)} %collective-permute-done.4, f32[4,256,192]{2,1,0:T(8,128)S(1)} %get-tuple-element.63, bf16[4,256,192]{2,1,0:T(8,128)(2,1)S(1)} %collective-permute-done.3), kind=kLoop, calls=%fused_computation | loop fusion | flops 983040 | bytes 1966080 | tf_op jit(solution)/shard_map/convert_element_type | solution.py:705
  71.2 7.0 %all-to-all-done.2 = bf16[16,80,128]{2,1,0:T(8,128)(2,1)S(1)} async-done(((bf16[16,80,128]{2,1,0:T(8,128)(2,1)}), bf16[16,80,128]{2,1,0:T(8,128)(2,1)S(1)}, u32[]{:S(2)}, u32[]{:S(2)}) %all-to-all-start.2) | async-done | bytes 327712 | tf_op jit(solution)/shard_map/all_to_all | solution.py:652
  78.7 1.3 %collective-permute-done.5.other_ref = bf16[1280,128]{1,0:T(8,128)(2,1)S(1)} collective-permute-done((bf16[1280,128]{1,0:T(8,128)(2,1)S(1)}, bf16[1280,128]{1,0:T(8,128)(2,1)S(1)}, u32[]{:S(2)}, u32[]{:S(2)}) %collective-permute-start.5) | collective-permute-done | bytes 327712 | tf_op jit(solution)/shard_map/ppermute | solution.py:708
  80.0 1.1 %shard_map.174 = (f32[192,768]{1,0:T(8,128)}, f32[192,768]{1,0:T(8,128)}, f32[7,7,192]{2,1,0:T(8,128)}, f32[192]{0:T(256)}, f32[192]{0:T(256)}, /*index=5*/f32[768]{0:T(1024)}) custom-call(s32[1]{0:T(128)} %bitcast.9.core_ref, bf16[1280,128]{1,0:T(8,128)(2,1)S(1)} %bitcast.13, bf16[1280,128]{1,0:T(8,128)(2,1)S(1)} %collective-permute-done.5.other_ref), custom_call_target="tpu_custom_call" | custom-call | flops 1000000 | bytes 2000000 | tf_op jit(solution)/shard_map/pallas_call | solution.py:633
  (18 shorter events, 4.8 us)
Async XLA Ops:
  0.6 10.3 %collective-permute-start = (bf16[4,256,192]{2,1,0:T(8,128)(2,1)}, bf16[4,256,192]{2,1,0:T(8,128)(2,1)S(1)}, u32[]{:S(2)}, u32[]{:S(2)}) collective-permute-start(bf16[4,256,192]{2,1,0:T(8,128)(2,1)} %bitcast.16), channel_id=1, source_target_pairs={{0,1},{1,2},{2,3},{3,4},{4,5},{5,6},{6,7},{7,8},{8,9},{9,10},{10,1... | collective-permute-start | bytes 1179656 | tf_op jit(solution)/shard_map/ppermute | solution.py:679
  3.7 9.1 %collective-permute-start.1 = (bf16[4,256,192]{2,1,0:T(8,128)(2,1)}, bf16[4,256,192]{2,1,0:T(8,128)(2,1)S(1)}, u32[]{:S(2)}, u32[]{:S(2)}) collective-permute-start(bf16[4,256,192]{2,1,0:T(8,128)(2,1)} %bitcast.17), channel_id=1, source_target_pairs={{1,0},{2,1},{3,2},{4,3},{5,4},{6,5},{7,6},{8,7},{9,8},{10,9},{11,1... | collective-permute-start | bytes 1179656 | tf_op jit(solution)/shard_map/ppermute | solution.py:680
  5.5 1.0 %copy-start = (bf16[192,768]{1,0:T(8,128)(2,1)S(1)}, bf16[192,768]{1,0:T(8,128)(2,1)}, u32[]{:S(2)}) copy-start(bf16[192,768]{1,0:T(8,128)(2,1)} %up_hbm.1) | copy-start | bytes 884740
  6.5 1.0 %copy-start.1 = (bf16[768,192]{0,1:T(8,128)(2,1)S(1)}, bf16[768,192]{0,1:T(8,128)(2,1)}, u32[]{:S(2)}) copy-start(bf16[768,192]{0,1:T(8,128)(2,1)} %param.17) | copy-start | bytes 884740
  7.4 0.8 %copy-start.2 = (f32[7,7,192]{2,1,0:T(8,128)S(1)}, f32[7,7,192]{2,1,0:T(8,128)}, u32[]{:S(2)}) copy-start(f32[7,7,192]{2,1,0:T(8,128)} %kernel_hbm.1) | copy-start | bytes 112900
  25.2 5.6 %collective-permute-start.2 = (bf16[1280,128]{1,0:T(8,128)(2,1)S(1)}, bf16[1280,128]{1,0:T(8,128)(2,1)S(1)}, u32[]{:S(2)}, u32[]{:S(2)}) collective-permute-start(bf16[1280,128]{1,0:T(8,128)(2,1)S(1)} %get-tuple-element.53), channel_id=1, source_target_pairs={{0,1},{1,0},{2,3},{3,2},{4,5},{5,4},{6,7},{7,6},{8,9},{9,8},{10,11... | collective-permute-start | bytes 983048 | tf_op jit(solution)/shard_map/ppermute | solution.py:691
  31.5 12.6 %all-to-all-start = ((bf16[16,80,128]{2,1,0:T(8,128)(2,1)}), bf16[16,80,128]{2,1,0:T(8,128)(2,1)S(1)}, u32[]{:S(2)}, u32[]{:S(2)}) async-start(bf16[16,80,128]{2,1,0:T(8,128)(2,1)} %bitcast.7), calls=%async_computation | async-start | bytes 655360 | tf_op jit(solution)/shard_map/all_to_all | solution.py:693
  40.3 1.2 %copy-start.3 = (f32[6,528,128]{2,1,0:T(8,128)}, f32[6,528,128]{2,1,0:T(8,128)S(1)}, u32[]{:S(2)}) copy-start(f32[6,528,128]{2,1,0:T(8,128)S(1)} %shard_map.172.dpad) | copy-start | bytes 4866052
  44.9 14.7 %all-to-all-start.1 = ((bf16[8,80,128]{2,1,0:T(8,128)(2,1)}), bf16[8,80,128]{2,1,0:T(8,128)(2,1)S(1)}, u32[]{:S(2)}, u32[]{:S(2)}) async-start(bf16[8,80,128]{2,1,0:T(8,128)(2,1)} %broadcast_in_dim.20), calls=%async_computation.1 | async-start | bytes 327680 | tf_op jit(solution)/shard_map/all_to_all | solution.py:652
  51.2 1.4 %copy-start.4 = (f32[6,528,128]{2,1,0:T(8,128)S(1)}, f32[6,528,128]{2,1,0:T(8,128)}, u32[]{:S(2)}) copy-start(f32[6,528,128]{2,1,0:T(8,128)} %copy-done.3) | copy-start | bytes 4866052
  59.6 10.7 %collective-permute-start.3 = (bf16[4,256,192]{2,1,0:T(8,128)(2,1)S(1)}, bf16[4,256,192]{2,1,0:T(8,128)(2,1)S(1)}, u32[]{:S(2)}, u32[]{:S(2)}) collective-permute-start(bf16[4,256,192]{2,1,0:T(8,128)(2,1)S(1)} %get-tuple-element.64), channel_id=1, source_target_pairs={{1,0},{2,1},{3,2},{4,3},{5,4},{6,5},{7,6},{8,7},{9,8},{10,9},{11,1... | collective-permute-start | bytes 1179656 | tf_op jit(solution)/shard_map/ppermute | solution.py:701
  62.9 7.3 %collective-permute-start.4 = (bf16[4,256,192]{2,1,0:T(8,128)(2,1)S(1)}, bf16[4,256,192]{2,1,0:T(8,128)(2,1)S(1)}, u32[]{:S(2)}, u32[]{:S(2)}) collective-permute-start(bf16[4,256,192]{2,1,0:T(8,128)(2,1)S(1)} %get-tuple-element.65), channel_id=1, source_target_pairs={{0,1},{1,2},{2,3},{3,4},{4,5},{5,6},{6,7},{7,8},{8,9},{9,10},{10,1... | collective-permute-start | bytes 1179656 | tf_op jit(solution)/shard_map/ppermute | solution.py:702
  63.9 14.3 %all-to-all-start.2 = ((bf16[16,80,128]{2,1,0:T(8,128)(2,1)}), bf16[16,80,128]{2,1,0:T(8,128)(2,1)S(1)}, u32[]{:S(2)}, u32[]{:S(2)}) async-start(bf16[16,80,128]{2,1,0:T(8,128)(2,1)} %broadcast_in_dim.21), calls=%async_computation.2 | async-start | bytes 655360 | tf_op jit(solution)/shard_map/all_to_all | solution.py:652
  78.2 1.8 %collective-permute-start.5 = (bf16[1280,128]{1,0:T(8,128)(2,1)S(1)}, bf16[1280,128]{1,0:T(8,128)(2,1)S(1)}, u32[]{:S(2)}, u32[]{:S(2)}) collective-permute-start(bf16[1280,128]{1,0:T(8,128)(2,1)S(1)} %bitcast.12), channel_id=1, source_target_pairs={{0,1},{1,0},{2,3},{3,2},{4,5},{5,4},{6,7},{7,6},{8,9},{9,8},{10,11... | collective-permute-start | bytes 983048 | tf_op jit(solution)/shard_map/ppermute | solution.py:708

commit v4 on v3

--- a/solution.py
+++ b/solution.py
@@ -159,8 +159,7 @@
     for tile in range(T):
         for slot in range(8):
             row = table_ref[16, table_ref[slot, ids[tile]]]
-            block = lax.rem(row // T - position + 1 + BLOCKS, BLOCKS)
-            where_ref[tile * 8 + slot] = block * T + lax.rem(row, T)
+            where_ref[tile * 8 + slot] = (row - first + T) & (BLOCKS * T - 1)
             where_ref[T * 8 + tile * 8 + slot] = table_ref[8 + slot, ids[tile]]
 
     own_ref[:, :, C:] = jnp.zeros((T, PX, 256 - C), BF16)
@@ -332,7 +331,7 @@
 
     CH = 64
 
-    @pl.loop(0, (T // 2) * (PX // CH), unroll=4)
+    @pl.loop(0, (T // 2) * (PX // CH), unroll=8)
     def _(step):
         pair = step // (PX // CH)
         rows = pl.ds(pl.multiple_of(lax.rem(step, PX // CH) * CH, CH), CH)
@@ -403,7 +402,7 @@
                     mix[pair * 3 + 1] += normed_grad[:, :128]
                     mix[pair * 3 + 2] = normed_grad[:, 128:]
 
-    @pl.loop(0, (T // 2) * (PX // CH), unroll=4)
+    @pl.loop(0, (T // 2) * (PX // CH), unroll=8)
     def _(step):
         pair = step // (PX // CH)
         start = pl.multiple_of(lax.rem(step, PX // CH) * CH, CH)

time: 81.7 us -> 81.2 us (level)
  transfers between devices with their start and end apart: 9 -> 9, of which waited for: 7 -> 7; matrix products, arithmetic and copies ran while one was open for 4% -> 4% of each run, Pallas kernels for 12% -> 13%
where the time goes in v4:
time: 81.2 us; the launch traced here: 80.6 us
  starting transfers between devices  26.5 us (33%)
  Pallas kernels  23.1 us (28%)
  waiting for transfers between devices  20.2 us (25%)
  local copies, waits for them, and re-layouts  6.8 us (8%)
  other arithmetic  3.3 us (4%)
    pallas_call x1, Pallas kernels, run_forward(): pl.pallas_call(forward_kernel, out_shape=(jax.ShapeDtypeStruct((T, PX, C)...  11.9 us
    all_to_all x2, waiting for transfers between devices, shared_with(): lax.all_to_all(jnp.broadcast_to(x[None], (count,) + x.shape), axes, 0, 0)  10.3 us
    all_to_all x2, starting transfers between devices, shared_with(): lax.all_to_all(jnp.broadcast_to(x[None], (count,) + x.shape), axes, 0, 0)  9.88 us
    unnamed x10, local copies, waits for them, and re-layouts  5.34 us
    all_to_all x1, starting transfers between devices, on_device(): mine = lax.all_to_all(mine.reshape(16, HALF // 16, 128), plane, 0, 0)  4.88 us
    ppermute x1, starting transfers between devices, on_device(): mine = (keep + lax.ppermute(send, 'c', swap).astype(F32)).astype(BF16)  4.31 us
    pallas_call x1, Pallas kernels, run_spread(): pl.pallas_call(spread_kernel, out_shape=jax.ShapeDtypeStruct((SLABS, 22 *...  3.88 us
    pallas_call x1, Pallas kernels, run_return(): pl.pallas_call(return_kernel, out_shape=(jax.ShapeDtypeStruct(tile, F32),...  3.57 us
  transfers between devices with their start and end apart: 9, of which 7 were waited for; matrix products, arithmetic and copies ran while one was open for 4% of the time, Pallas kernels for 13%

profile of v4, /device:TPU:1, one launch (start us, length us, event | category | flops | bytes accessed | tf_op | source)
XLA Modules:
  0.0 80.6 jit_solution(3741187657323743542)
XLA Ops:
  0.6 3.1 %collective-permute-start = (bf16[4,256,192]{2,1,0:T(8,128)(2,1)}, bf16[4,256,192]{2,1,0:T(8,128)(2,1)S(1)}, u32[]{:S(2)}, u32[]{:S(2)}) collective-permute-start(bf16[4,256,192]{2,1,0:T(8,128)(2,1)} %bitcast.16), channel_id=1, source_target_pairs={{0,1},{1,2},{2,3},{3,4},{4,5},{5,6},{6,7},{7,8},{8,9},{9,10},{10,1... | collective-permute-start | bytes 1179656 | tf_op jit(solution)/shard_map/ppermute | solution.py:678
  5.5 1.0 %copy-done = bf16[192,768]{1,0:T(8,128)(2,1)S(1)} copy-done((bf16[192,768]{1,0:T(8,128)(2,1)S(1)}, bf16[192,768]{1,0:T(8,128)(2,1)}, u32[]{:S(2)}) %copy-start) | copy-done | bytes 294936
  6.5 1.0 %copy-done.1 = bf16[768,192]{0,1:T(8,128)(2,1)S(1)} copy-done((bf16[768,192]{0,1:T(8,128)(2,1)S(1)}, bf16[768,192]{0,1:T(8,128)(2,1)}, u32[]{:S(2)}) %copy-start.1) | copy-done | bytes 294936
  7.4 0.8 %copy-done.2 = f32[7,7,192]{2,1,0:T(8,128)S(1)} copy-done((f32[7,7,192]{2,1,0:T(8,128)S(1)}, f32[7,7,192]{2,1,0:T(8,128)}, u32[]{:S(2)}) %copy-start.2) | copy-done | bytes 37656
  8.2 2.7 %shard_map.170 = (s32[64]{0:T(128)S(1)}, bf16[4,256,256]{2,1,0:T(8,128)(2,1)S(1)}, bf16[4,256,192]{2,1,0:T(8,128)(2,1)S(1)}, bf16[192,768]{1,0:T(8,128)(2,1)S(1)...) custom-call(s32[17,128]{1,0:T(8,128)S(1)} %pad_add_fusion.table_ref,, ...), custom_call_target="tpu_custom_call" | custom-call | flops 100000000 | bytes 6000000 | tf_op jit(solution)/shard_map/pallas_call | solution.py:184
  10.9 1.9 %collective-permute-done.1.next_ref = bf16[4,256,192]{2,1,0:T(8,128)(2,1)S(1)} collective-permute-done((bf16[4,256,192]{2,1,0:T(8,128)(2,1)}, bf16[4,256,192]{2,1,0:T(8,128)(2,1)S(1)}, u32[]{:S(2)}, u32[]{:S(2)}) %collective-permute-start.1) | collective-permute-done | bytes 393248 | tf_op jit(solution)/shard_map/ppermute | solution.py:679
  12.8 11.9 %shard_map.171 = (bf16[4,256,192]{2,1,0:T(8,128)(2,1)}, f32[6,512,128]{2,1,0:T(8,128)S(1)}, bf16[1280,128]{1,0:T(8,128)(2,1)S(1)}, f32[1280,128]{1,0:T(8,128)S(1)}) custom-call(s32[64]{0:T(128)S(1)} %get-tuple-element.41.where_ref, bf16[4,256,192]{2,1,0:T(8,128)(2,1)S(1)} %collective-permute-done.prev_ref, ...), custom_call_target="tpu_custom_call" | custom-call | flops 4000000000 | bytes 8000000 | tf_op jit(solution)/shard_map/pallas_call | solution.py:472
  24.7 4.3 %collective-permute-start.2 = (bf16[1280,128]{1,0:T(8,128)(2,1)S(1)}, bf16[1280,128]{1,0:T(8,128)(2,1)S(1)}, u32[]{:S(2)}, u32[]{:S(2)}) collective-permute-start(bf16[1280,128]{1,0:T(8,128)(2,1)S(1)} %get-tuple-element.53), channel_id=1, source_target_pairs={{0,1},{1,0},{2,3},{3,2},{4,5},{5,4},{6,7},{7,6},{8,9},{9,8},{10,11... | collective-permute-start | bytes 983048 | tf_op jit(solution)/shard_map/ppermute | solution.py:690
  29.0 1.3 %collective-permute-done.2 = bf16[1280,128]{1,0:T(8,128)(2,1)S(1)} collective-permute-done((bf16[1280,128]{1,0:T(8,128)(2,1)S(1)}, bf16[1280,128]{1,0:T(8,128)(2,1)S(1)}, u32[]{:S(2)}, u32[]{:S(2)}) %collective-permute-start.2) | collective-permute-done | bytes 327712 | tf_op jit(solution)/shard_map/ppermute | solution.py:690
  31.1 4.9 %all-to-all-start = ((bf16[16,80,128]{2,1,0:T(8,128)(2,1)}), bf16[16,80,128]{2,1,0:T(8,128)(2,1)S(1)}, u32[]{:S(2)}, u32[]{:S(2)}) async-start(bf16[16,80,128]{2,1,0:T(8,128)(2,1)} %bitcast.7), calls=%async_computation | async-start | bytes 655360 | tf_op jit(solution)/shard_map/all_to_all | solution.py:692
  36.0 3.9 %shard_map.172.dpad = f32[6,528,128]{2,1,0:T(8,128)S(1)} custom-call(f32[6,512,128]{2,1,0:T(8,128)S(1)} %get-tuple-element.54.dmix, f32[3,56,128]{2,1,0:T(8,128)S(1)} %get-tuple-element.46.taps_ref), custom_call_target="tpu_custom_call" | custom-call | flops 1000000000 | bytes 5000000 | tf_op jit(solution)/shard_map/pallas_call | solution.py:528
  39.9 1.2 %copy-done.3 = f32[6,528,128]{2,1,0:T(8,128)} copy-done((f32[6,528,128]{2,1,0:T(8,128)}, f32[6,528,128]{2,1,0:T(8,128)S(1)}, u32[]{:S(2)}) %copy-start.3) | copy-done | bytes 1622040
  41.0 2.7 %all-to-all-done = bf16[16,80,128]{2,1,0:T(8,128)(2,1)S(1)} async-done(((bf16[16,80,128]{2,1,0:T(8,128)(2,1)}), bf16[16,80,128]{2,1,0:T(8,128)(2,1)S(1)}, u32[]{:S(2)}, u32[]{:S(2)}) %all-to-all-start) | async-done | bytes 327712 | tf_op jit(solution)/shard_map/all_to_all | solution.py:692
  44.4 6.3 %all-to-all-start.1 = ((bf16[8,80,128]{2,1,0:T(8,128)(2,1)}), bf16[8,80,128]{2,1,0:T(8,128)(2,1)S(1)}, u32[]{:S(2)}, u32[]{:S(2)}) async-start(bf16[8,80,128]{2,1,0:T(8,128)(2,1)} %broadcast_in_dim.20), calls=%async_computation.1 | async-start | bytes 327680 | tf_op jit(solution)/shard_map/all_to_all | solution.py:651
  50.8 1.4 %copy-done.4 = f32[6,528,128]{2,1,0:T(8,128)S(1)} copy-done((f32[6,528,128]{2,1,0:T(8,128)S(1)}, f32[6,528,128]{2,1,0:T(8,128)}, u32[]{:S(2)}) %copy-start.4) | copy-done | bytes 1622040
  52.2 3.6 %shard_map.173 = (f32[4,256,192]{2,1,0:T(8,128)S(1)}, bf16[4,256,192]{2,1,0:T(8,128)(2,1)S(1)}, bf16[4,256,192]{2,1,0:T(8,128)(2,1)S(1)}) custom-call(s32[64]{0:T(128)S(1)} %get-tuple-element.41.where_ref, f32[6,528,128]{2,1,0:T(8,128)S(1)} %copy-done.4, bf16[4,256,192]{2,1,0:T(8,128)(2,1)S(1)} %get-tuple-element.43.cot_ref), custom_call_target="tpu_custom_call" | custom-call | flops 1000000000 | bytes 5000000 | tf_op jit(solution)/shard_map/pallas_call | solution.py:584
  55.8 3.4 %all-to-all-done.1 = bf16[8,80,128]{2,1,0:T(8,128)(2,1)S(1)} async-done(((bf16[8,80,128]{2,1,0:T(8,128)(2,1)}), bf16[8,80,128]{2,1,0:T(8,128)(2,1)S(1)}, u32[]{:S(2)}, u32[]{:S(2)}) %all-to-all-start.1) | async-done | bytes 163872 | tf_op jit(solution)/shard_map/all_to_all | solution.py:651
  59.2 3.3 %collective-permute-start.3 = (bf16[4,256,192]{2,1,0:T(8,128)(2,1)S(1)}, bf16[4,256,192]{2,1,0:T(8,128)(2,1)S(1)}, u32[]{:S(2)}, u32[]{:S(2)}) collective-permute-start(bf16[4,256,192]{2,1,0:T(8,128)(2,1)S(1)} %get-tuple-element.64), channel_id=1, source_target_pairs={{1,0},{2,1},{3,2},{4,3},{5,4},{6,5},{7,6},{8,7},{9,8},{10,9},{11,1... | collective-permute-start | bytes 1179656 | tf_op jit(solution)/shard_map/ppermute | solution.py:700
  63.5 3.5 %all-to-all-start.2 = ((bf16[16,80,128]{2,1,0:T(8,128)(2,1)}), bf16[16,80,128]{2,1,0:T(8,128)(2,1)S(1)}, u32[]{:S(2)}, u32[]{:S(2)}) async-start(bf16[16,80,128]{2,1,0:T(8,128)(2,1)} %broadcast_in_dim.21), calls=%async_computation.2 | async-start | bytes 655360 | tf_op jit(solution)/shard_map/all_to_all | solution.py:651
  67.0 2.8 %collective-permute-done.3 = bf16[4,256,192]{2,1,0:T(8,128)(2,1)S(1)} collective-permute-done((bf16[4,256,192]{2,1,0:T(8,128)(2,1)S(1)}, bf16[4,256,192]{2,1,0:T(8,128)(2,1)S(1)}, u32[]{:S(2)}, u32[]{:S(2)}) %collective-permute-start.3) | collective-permute-done | bytes 393248 | tf_op jit(solution)/shard_map/ppermute | solution.py:700
  69.8 1.0 %add_convert_fusion = bf16[4,256,192]{2,1,0:T(8,128)(2,1)} fusion(bf16[4,256,192]{2,1,0:T(8,128)(2,1)S(1)} %collective-permute-done.4, f32[4,256,192]{2,1,0:T(8,128)S(1)} %get-tuple-element.63, bf16[4,256,192]{2,1,0:T(8,128)(2,1)S(1)} %collective-permute-done.3), kind=kLoop, calls=%fused_computation | loop fusion | flops 983040 | bytes 1966080 | tf_op jit(solution)/shard_map/convert_element_type | solution.py:704
  70.8 7.0 %all-to-all-done.2 = bf16[16,80,128]{2,1,0:T(8,128)(2,1)S(1)} async-done(((bf16[16,80,128]{2,1,0:T(8,128)(2,1)}), bf16[16,80,128]{2,1,0:T(8,128)(2,1)S(1)}, u32[]{:S(2)}, u32[]{:S(2)}) %all-to-all-start.2) | async-done | bytes 327712 | tf_op jit(solution)/shard_map/all_to_all | solution.py:651
  78.3 1.3 %collective-permute-done.5.other_ref = bf16[1280,128]{1,0:T(8,128)(2,1)S(1)} collective-permute-done((bf16[1280,128]{1,0:T(8,128)(2,1)S(1)}, bf16[1280,128]{1,0:T(8,128)(2,1)S(1)}, u32[]{:S(2)}, u32[]{:S(2)}) %collective-permute-start.5) | collective-permute-done | bytes 327712 | tf_op jit(solution)/shard_map/ppermute | solution.py:707
  79.5 1.1 %shard_map.174 = (f32[192,768]{1,0:T(8,128)}, f32[192,768]{1,0:T(8,128)}, f32[7,7,192]{2,1,0:T(8,128)}, f32[192]{0:T(256)}, f32[192]{0:T(256)}, /*index=5*/f32[768]{0:T(1024)}) custom-call(s32[1]{0:T(128)} %bitcast.9.core_ref, bf16[1280,128]{1,0:T(8,128)(2,1)S(1)} %bitcast.13, bf16[1280,128]{1,0:T(8,128)(2,1)S(1)} %collective-permute-done.5.other_ref), custom_call_target="tpu_custom_call" | custom-call | flops 1000000 | bytes 2000000 | tf_op jit(solution)/shard_map/pallas_call | solution.py:632
  (18 shorter events, 4.8 us)
Async XLA Ops:
  0.6 10.3 %collective-permute-start = (bf16[4,256,192]{2,1,0:T(8,128)(2,1)}, bf16[4,256,192]{2,1,0:T(8,128)(2,1)S(1)}, u32[]{:S(2)}, u32[]{:S(2)}) collective-permute-start(bf16[4,256,192]{2,1,0:T(8,128)(2,1)} %bitcast.16), channel_id=1, source_target_pairs={{0,1},{1,2},{2,3},{3,4},{4,5},{5,6},{6,7},{7,8},{8,9},{9,10},{10,1... | collective-permute-start | bytes 1179656 | tf_op jit(solution)/shard_map/ppermute | solution.py:678
  3.7 9.1 %collective-permute-start.1 = (bf16[4,256,192]{2,1,0:T(8,128)(2,1)}, bf16[4,256,192]{2,1,0:T(8,128)(2,1)S(1)}, u32[]{:S(2)}, u32[]{:S(2)}) collective-permute-start(bf16[4,256,192]{2,1,0:T(8,128)(2,1)} %bitcast.17), channel_id=1, source_target_pairs={{1,0},{2,1},{3,2},{4,3},{5,4},{6,5},{7,6},{8,7},{9,8},{10,9},{11,1... | collective-permute-start | bytes 1179656 | tf_op jit(solution)/shard_map/ppermute | solution.py:679
  5.5 1.0 %copy-start = (bf16[192,768]{1,0:T(8,128)(2,1)S(1)}, bf16[192,768]{1,0:T(8,128)(2,1)}, u32[]{:S(2)}) copy-start(bf16[192,768]{1,0:T(8,128)(2,1)} %up_hbm.1) | copy-start | bytes 884740
  6.5 1.0 %copy-start.1 = (bf16[768,192]{0,1:T(8,128)(2,1)S(1)}, bf16[768,192]{0,1:T(8,128)(2,1)}, u32[]{:S(2)}) copy-start(bf16[768,192]{0,1:T(8,128)(2,1)} %param.17) | copy-start | bytes 884740
  7.4 0.8 %copy-start.2 = (f32[7,7,192]{2,1,0:T(8,128)S(1)}, f32[7,7,192]{2,1,0:T(8,128)}, u32[]{:S(2)}) copy-start(f32[7,7,192]{2,1,0:T(8,128)} %kernel_hbm.1) | copy-start | bytes 112900
  24.7 5.6 %collective-permute-start.2 = (bf16[1280,128]{1,0:T(8,128)(2,1)S(1)}, bf16[1280,128]{1,0:T(8,128)(2,1)S(1)}, u32[]{:S(2)}, u32[]{:S(2)}) collective-permute-start(bf16[1280,128]{1,0:T(8,128)(2,1)S(1)} %get-tuple-element.53), channel_id=1, source_target_pairs={{0,1},{1,0},{2,3},{3,2},{4,5},{5,4},{6,7},{7,6},{8,9},{9,8},{10,11... | collective-permute-start | bytes 983048 | tf_op jit(solution)/shard_map/ppermute | solution.py:690
  31.1 12.6 %all-to-all-start = ((bf16[16,80,128]{2,1,0:T(8,128)(2,1)}), bf16[16,80,128]{2,1,0:T(8,128)(2,1)S(1)}, u32[]{:S(2)}, u32[]{:S(2)}) async-start(bf16[16,80,128]{2,1,0:T(8,128)(2,1)} %bitcast.7), calls=%async_computation | async-start | bytes 655360 | tf_op jit(solution)/shard_map/all_to_all | solution.py:692
  39.9 1.2 %copy-start.3 = (f32[6,528,128]{2,1,0:T(8,128)}, f32[6,528,128]{2,1,0:T(8,128)S(1)}, u32[]{:S(2)}) copy-start(f32[6,528,128]{2,1,0:T(8,128)S(1)} %shard_map.172.dpad) | copy-start | bytes 4866052
  44.4 14.7 %all-to-all-start.1 = ((bf16[8,80,128]{2,1,0:T(8,128)(2,1)}), bf16[8,80,128]{2,1,0:T(8,128)(2,1)S(1)}, u32[]{:S(2)}, u32[]{:S(2)}) async-start(bf16[8,80,128]{2,1,0:T(8,128)(2,1)} %broadcast_in_dim.20), calls=%async_computation.1 | async-start | bytes 327680 | tf_op jit(solution)/shard_map/all_to_all | solution.py:651
  50.8 1.4 %copy-start.4 = (f32[6,528,128]{2,1,0:T(8,128)S(1)}, f32[6,528,128]{2,1,0:T(8,128)}, u32[]{:S(2)}) copy-start(f32[6,528,128]{2,1,0:T(8,128)} %copy-done.3) | copy-start | bytes 4866052
  59.2 10.7 %collective-permute-start.3 = (bf16[4,256,192]{2,1,0:T(8,128)(2,1)S(1)}, bf16[4,256,192]{2,1,0:T(8,128)(2,1)S(1)}, u32[]{:S(2)}, u32[]{:S(2)}) collective-permute-start(bf16[4,256,192]{2,1,0:T(8,128)(2,1)S(1)} %get-tuple-element.64), channel_id=1, source_target_pairs={{1,0},{2,1},{3,2},{4,3},{5,4},{6,5},{7,6},{8,7},{9,8},{10,9},{11,1... | collective-permute-start | bytes 1179656 | tf_op jit(solution)/shard_map/ppermute | solution.py:700
  62.5 7.3 %collective-permute-start.4 = (bf16[4,256,192]{2,1,0:T(8,128)(2,1)S(1)}, bf16[4,256,192]{2,1,0:T(8,128)(2,1)S(1)}, u32[]{:S(2)}, u32[]{:S(2)}) collective-permute-start(bf16[4,256,192]{2,1,0:T(8,128)(2,1)S(1)} %get-tuple-element.65), channel_id=1, source_target_pairs={{0,1},{1,2},{2,3},{3,4},{4,5},{5,6},{6,7},{7,8},{8,9},{9,10},{10,1... | collective-permute-start | bytes 1179656 | tf_op jit(solution)/shard_map/ppermute | solution.py:701
  63.5 14.3 %all-to-all-start.2 = ((bf16[16,80,128]{2,1,0:T(8,128)(2,1)}), bf16[16,80,128]{2,1,0:T(8,128)(2,1)S(1)}, u32[]{:S(2)}, u32[]{:S(2)}) async-start(bf16[16,80,128]{2,1,0:T(8,128)(2,1)} %broadcast_in_dim.21), calls=%async_computation.2 | async-start | bytes 655360 | tf_op jit(solution)/shard_map/all_to_all | solution.py:651
  77.7 1.8 %collective-permute-start.5 = (bf16[1280,128]{1,0:T(8,128)(2,1)S(1)}, bf16[1280,128]{1,0:T(8,128)(2,1)S(1)}, u32[]{:S(2)}, u32[]{:S(2)}) collective-permute-start(bf16[1280,128]{1,0:T(8,128)(2,1)S(1)} %bitcast.12), channel_id=1, source_target_pairs={{0,1},{1,0},{2,3},{3,2},{4,5},{5,4},{6,7},{7,6},{8,9},{9,8},{10,11... | collective-permute-start | bytes 983048 | tf_op jit(solution)/shard_map/ppermute | solution.py:707
